TPU v7x, 256 devices: a whole 4x4x8 slice. The times are simulated.
256 devices in a mesh: gx: 32 (over y, z), gy: 8 (over x, core).
Axes of the slice: x: 4, y: 4, z: 8, core: 2. Of those that a mesh axis runs over, the one named last changes fastest.
Arguments:
- tokens: bfloat16 [1, 512, 512, 128], P(None, 'gx', 'gy'), may hold values from -6 to 6
- norm_gain: float32 [128], replicated, may hold values from 0.1 to 1.9
- qkv_weight: bfloat16 [128, 384], replicated, may hold values from -0.5 to 0.5
- output_weight: bfloat16 [128, 128], replicated, may hold values from -0.5 to 0.5
- cotangent: bfloat16 [1, 512, 512, 128], P(None, 'gx', 'gy'), may hold values from -6 to 6
Outputs:
- block_output: bfloat16 [1, 512, 512, 128], P(None, 'gx', 'gy')
- token_grads: bfloat16 [1, 512, 512, 128], P(None, 'gx', 'gy')
- qkv_grads: float32 [128, 384], replicated
- output_grads: float32 [128, 128], replicated
- gain_grads: float32 [128], replicated
All inputs are finite; a program needn't handle non-finite values.
Results may differ from a plain program's by a relative error of at most 0.0096.
Values may be sent and summed in bfloat16 or wider, within the bound.
A program may use at most 64 MiB of HBM per device.

v0:
```python
import jax
import jax.numpy as jnp
from jax import lax
from jax.sharding import PartitionSpec as P

HEADS = 2


EPS = 1e-06


def padded_2(x, sides, width):
    for axis, dim in sides:
        size, length = (lax.axis_size(axis), x.shape[dim])
        up = [(i, (i + 1) % size) for i in range(size - 1)]
        down = [(j, i) for i, j in up]
        last = lax.slice_in_dim(x, length - width, length, axis=dim)
        first = lax.slice_in_dim(x, 0, width, axis=dim)
        before = lax.ppermute(last, axis, up)
        after = lax.ppermute(first, axis, down)
        x = jnp.concatenate([before, x, after], axis=dim)
    return x


def to_blocks(values_in, tile_rows, tile_cols):
    features = values_in.shape[-1]
    shaped = values_in.reshape(tile_rows // 8, 8, tile_cols // 8, 8, features)
    return shaped.transpose(0, 2, 1, 3, 4).reshape(tile_rows // 8, tile_cols // 8, 64, features)


def from_blocks(blocks, tile_rows, tile_cols):
    features = blocks.shape[-1]
    shaped = blocks.reshape(tile_rows // 8, tile_cols // 8, 8, 8, features)
    return shaped.transpose(0, 2, 1, 3, 4).reshape(tile_rows, tile_cols, features)


def to_windows(values_in, tile_rows, tile_cols):
    features = values_in.shape[-1]
    block_rows = tile_rows // 8
    block_cols = tile_cols // 8
    upper_half = values_in[0:tile_rows].reshape(block_rows, 8, tile_cols + 8, features)
    lower_half = values_in[8 : tile_rows + 8].reshape(block_rows, 8, tile_cols + 8, features)
    banded = jnp.concatenate([upper_half, lower_half], axis=1)
    left_half = banded[:, :, 0:tile_cols].reshape(block_rows, 16, block_cols, 8, features)
    right_half = banded[:, :, 8 : tile_cols + 8].reshape(block_rows, 16, block_cols, 8, features)
    window_tiles = jnp.concatenate([left_half, right_half], axis=3)
    return window_tiles.transpose(0, 2, 1, 3, 4).reshape(block_rows, block_cols, 256, features)


def from_windows(window_tiles, tile_rows, tile_cols):
    features = window_tiles.shape[-1]
    block_rows = tile_rows // 8
    block_cols = tile_cols // 8
    shaped = window_tiles.reshape(block_rows, block_cols, 16, 16, features).transpose(0, 2, 1, 3, 4)
    left_half = shaped[:, :, :, 0:8].reshape(block_rows, 16, tile_cols, features)
    right_half = shaped[:, :, :, 8:16].reshape(block_rows, 16, tile_cols, features)
    banded = jnp.pad(left_half, ((0, 0), (0, 0), (0, 8), (0, 0))) + jnp.pad(
        right_half, ((0, 0), (0, 0), (8, 0), (0, 0))
    )
    upper_half = banded[:, 0:8].reshape(tile_rows, tile_cols + 8, features)
    lower_half = banded[:, 8:16].reshape(tile_rows, tile_cols + 8, features)
    return jnp.pad(upper_half, ((0, 8), (0, 0), (0, 0))) + jnp.pad(
        lower_half, ((8, 0), (0, 0), (0, 0))
    )


def window_mask(tile_rows, tile_cols, row_start, col_start, image_height, image_width):
    centre = jnp.arange(64, dtype=jnp.int32)
    beside_all = jnp.arange(256, dtype=jnp.int32)
    row_gap = beside_all[None, :] // 16 - centre[:, None] // 8
    col_gap = beside_all[None, :] % 16 - centre[:, None] % 8
    near_mask = ((row_gap >= 1) & (row_gap <= 7) & (col_gap >= 1) & (col_gap <= 7)).astype(
        jnp.float32
    )
    global_row = (
        row_start
        - 4
        + jnp.arange(tile_rows // 8, dtype=jnp.int32)[:, None] * 8
        + beside_all[None, :] // 16
    )
    global_col = (
        col_start
        - 4
        + jnp.arange(tile_cols // 8, dtype=jnp.int32)[:, None] * 8
        + beside_all[None, :] % 16
    )
    row_inside = ((global_row >= 0) & (global_row < image_height)).astype(jnp.float32)
    col_inside = ((global_col >= 0) & (global_col < image_width)).astype(jnp.float32)
    inside = row_inside[:, None, :] * col_inside[None, :, :]
    return (near_mask[None, None] * inside[:, :, None, :], inside)


def split_heads(values_in, head_count):
    return values_in.reshape(values_in.shape[:-1] + (head_count, values_in.shape[-1] // head_count))


def query_side(query, keyval, d_attended, window_on, tile_rows, tile_cols, head_count):
    channels = query.shape[-1]
    block_rows = tile_rows // 8
    block_cols = tile_cols // 8
    query_blocks = split_heads(to_blocks(query, tile_rows, tile_cols), head_count)
    windows = to_windows(keyval, tile_rows, tile_cols)
    key_windows = split_heads(windows[..., :channels], head_count)
    value_windows = split_heads(windows[..., channels:], head_count)
    scores = jnp.einsum(
        "xyqhd,xykhd->xyhqk", query_blocks, key_windows, preferred_element_type=jnp.float32
    )
    weights = jnp.exp(scores) * window_on[:, :, None]
    totals = jnp.sum(weights, axis=-1)
    shares = weights / totals[..., None]
    shares_low = shares.astype(jnp.bfloat16)
    attended = jnp.einsum(
        "xyhqk,xykhd->xyqhd", shares_low, value_windows, preferred_element_type=jnp.float32
    )
    grad_blocks = split_heads(to_blocks(d_attended, tile_rows, tile_cols), head_count)
    d_shares = jnp.einsum(
        "xyqhd,xykhd->xyhqk", grad_blocks, value_windows, preferred_element_type=jnp.float32
    )
    delta_sum = jnp.sum(shares * d_shares, axis=-1)
    d_scores = (shares * (d_shares - delta_sum[..., None])).astype(jnp.bfloat16)
    d_query = jnp.einsum(
        "xyhqk,xykhd->xyqhd", d_scores, key_windows, preferred_element_type=jnp.float32
    )
    attended = from_blocks(
        attended.reshape(block_rows, block_cols, 64, channels), tile_rows, tile_cols
    ).astype(jnp.bfloat16)
    d_query = from_blocks(
        d_query.reshape(block_rows, block_cols, 64, channels), tile_rows, tile_cols
    )
    statistics = jnp.concatenate([totals, delta_sum], axis=2).transpose(0, 1, 3, 2)
    statistics = from_blocks(statistics, tile_rows, tile_cols)
    d_key = jnp.einsum(
        "xyhqk,xyqhd->xykhd", d_scores, query_blocks, preferred_element_type=jnp.float32
    )
    d_value = jnp.einsum(
        "xyhqk,xyqhd->xykhd", shares_low, grad_blocks, preferred_element_type=jnp.float32
    )
    joined = jnp.concatenate(
        [
            d_key.reshape(block_rows, block_cols, 256, channels),
            d_value.reshape(block_rows, block_cols, 256, channels),
        ],
        axis=-1,
    )
    return (attended, d_query, statistics, from_windows(joined, tile_rows, tile_cols))


def fold_back(beside_all, tile_rows, tile_cols):
    core_rows = beside_all[:, 6 : tile_rows + 6]
    core_rows = core_rows.at[:, 0:3].add(beside_all[:, 0:3])
    core_rows = core_rows.at[:, tile_rows - 3 : tile_rows].add(
        beside_all[:, tile_rows + 9 : tile_rows + 12]
    )
    result = core_rows[:, :, 6 : tile_cols + 6]
    result = result.at[:, :, 0:3].add(core_rows[:, :, 0:3])
    result = result.at[:, :, tile_cols - 3 : tile_cols].add(
        core_rows[:, :, tile_cols + 9 : tile_cols + 12]
    )
    return result


def per_device(tokens, norm_gain, qkv_weight, output_weight, cotangent):
    batch_count, tile_rows, tile_cols, channels = tokens.shape
    head_count = HEADS
    q_scale = (channels // head_count) ** (-0.5)
    image_height = tile_rows * lax.axis_size("gx")
    image_width = tile_cols * lax.axis_size("gy")
    row_start = lax.axis_index("gx") * tile_rows
    col_start = lax.axis_index("gy") * tile_cols
    flat_tokens = tokens.reshape(-1, channels).astype(jnp.float32)
    flat_grads = cotangent.reshape(-1, channels)
    inverse_rms = lax.rsqrt(jnp.mean(flat_tokens * flat_tokens, axis=-1, keepdims=True) + EPS)
    unit_rows = flat_tokens * inverse_rms
    normed = (unit_rows * norm_gain).astype(jnp.bfloat16)
    projected = jnp.dot(normed, qkv_weight, preferred_element_type=jnp.float32)
    query = (
        (projected[:, :channels] * q_scale)
        .astype(jnp.bfloat16)
        .reshape(batch_count, tile_rows, tile_cols, channels)
    )
    keyval = (
        projected[:, channels:]
        .astype(jnp.bfloat16)
        .reshape(batch_count, tile_rows, tile_cols, 2 * channels)
    )
    d_attended = lax.dot_general(
        flat_grads, output_weight, (((1,), (1,)), ((), ())), preferred_element_type=jnp.float32
    )
    d_attended = d_attended.astype(jnp.bfloat16).reshape(
        batch_count, tile_rows, tile_cols, channels
    )
    rims = padded_2(keyval, (("gx", 1), ("gy", 2)), 3)
    padded = jnp.pad(rims, ((0, 0), (1, 1), (1, 1), (0, 0)))
    window_on, inside = window_mask(
        tile_rows, tile_cols, row_start, col_start, image_height, image_width
    )

    def per_image(image_items):
        return query_side(
            image_items[0],
            image_items[1],
            image_items[2],
            window_on,
            tile_rows,
            tile_cols,
            head_count,
        )

    attended, d_query, statistics, d_keys = lax.map(per_image, (query, padded, d_attended))
    inner = d_keys[:, 1 : tile_rows + 7, 1 : tile_cols + 7]
    beside_all = padded_2(inner.astype(jnp.bfloat16), (("gx", 1), ("gy", 2)), 3).astype(inner.dtype)
    d_keyval = fold_back(beside_all, tile_rows, tile_cols)
    flat_attended = attended.reshape(-1, channels)
    mixed_rows = flat_tokens + jnp.dot(
        flat_attended, output_weight, preferred_element_type=jnp.float32
    )
    block_output = mixed_rows.astype(jnp.bfloat16).reshape(tokens.shape)
    d_projected = (
        jnp.concatenate([d_query * q_scale, d_keyval], axis=-1)
        .astype(jnp.bfloat16)
        .reshape(-1, 3 * channels)
    )
    d_normed = lax.dot_general(
        d_projected, qkv_weight, (((1,), (1,)), ((), ())), preferred_element_type=jnp.float32
    )
    scaled_grad = d_normed * norm_gain
    d_flat = flat_grads.astype(jnp.float32) + inverse_rms * (
        scaled_grad - unit_rows * jnp.mean(scaled_grad * unit_rows, axis=-1, keepdims=True)
    )
    token_grads = d_flat.astype(jnp.bfloat16).reshape(tokens.shape)
    local_qkv = lax.dot_general(
        normed, d_projected, (((0,), (0,)), ((), ())), preferred_element_type=jnp.float32
    )
    local_output = lax.dot_general(
        flat_attended, flat_grads, (((0,), (0,)), ((), ())), preferred_element_type=jnp.float32
    )
    local_gain = jnp.sum(d_normed * unit_rows, axis=0)
    summed_qkv, summed_output, summed_gain = lax.psum(
        (local_qkv, local_output, local_gain), ("gx", "gy")
    )
    factor = (batch_count * image_height * image_width) ** (-0.5)
    return (
        block_output,
        token_grads,
        summed_qkv * factor,
        summed_output * factor,
        summed_gain * factor,
    )


def solution(mesh):
    in_specs = (P(None, "gx", "gy", None), P(), P(), P(), P(None, "gx", "gy", None))
    out_specs = (P(None, "gx", "gy", None), P(None, "gx", "gy", None), P(), P(), P())
    return jax.shard_map(
        per_device, mesh=mesh, in_specs=in_specs, out_specs=out_specs, check_vma=False
    )
```

profile of v0, /device:TPU:1, one launch (start us, length us, event | category | flops | bytes accessed | tf_op | source)
XLA Modules:
  0.0 432.4 jit_solution(16536356409240740789)
XLA Ops:
  7.2 1.2 multiply_reduce_fusion.3
  8.5 1.2 multiply_convert_fusion.1
  11.5 5.0 %collective-permute-start = (bf16[1,3,64,256]{3,2,1,0:T(8,128)(2,1)}, bf16[1,3,64,256]{3,2,1,0:T(8,128)(2,1)}, u32[]{:S(2)}, u32[]{:S(2)}) collective-permute-start(bf16[1,3,64,256]{3,2,1,0:T(8,128)(2,1)} %get-tuple-element.97), channel_id=1, source_target_pairs={{0,8},{8,16},{16,24},{24,32},{32,40},{40,48},{48,56},{56,64},{64,7... | collective-permute-start | bytes 294920 | tf_op jit(solution)/shard_map/ppermute | solution.py:19
  16.5 1.3 collective-permute-start.1
  18.9 3.2 collective-permute-done.1
  22.1 1.4 pad_maximum_fusion.9
  23.6 5.1 %collective-permute-start.2 = (bf16[1,22,3,256]{3,2,1,0:T(4,128)(2,1)}, bf16[1,22,3,256]{3,2,1,0:T(4,128)(2,1)}, u32[]{:S(2)}, u32[]{:S(2)}) collective-permute-start(bf16[1,22,3,256]{3,2,1,0:T(4,128)(2,1)} %get-tuple-element.95), channel_id=1, source_target_pairs={{0,1},{1,2},{2,3},{3,4},{4,5},{5,6},{6,7},{8,9},{9,10},{10,11},{11... | collective-permute-start | bytes 101384 | tf_op jit(solution)/shard_map/ppermute | solution.py:19
  28.7 1.9 collective-permute-start.3
  32.4 2.0 collective-permute-done.3
  34.4 1.4 select_maximum_fusion
  36.4 1.9 fusion.42
  38.4 1.5 copy.34
  39.8 2.3 copy.32
  43.3 1.5 fusion.6
  44.9 1.2 multiply_reduce_fusion
  46.1 2.0 convolution_bitcast_fusion
  49.7 1.3 copy.36
  51.3 4.3 %copy.43 = f32[2,8,256,2,64]{4,3,2,1,0:T(2,128)} copy(f32[2,8,256,2,64]{2,4,3,1,0:T(8,128)S(1)} %convolution_bitcast_fusion.1) | data formatting | bytes 4194304 | tf_op jit(solution)/shard_map/while/body/eval_jaxpr/xyhqk,xyqhd->xykhd/transpose | solution.py:132
  55.7 4.3 concatenate.58
  60.0 6.7 %copy.45 = f32[2,8,256,2,64]{4,3,2,1,0:T(2,128)} copy(f32[2,8,256,2,64]{2,4,3,1,0:T(8,128)} %convolution_bitcast_fusion) | data formatting | bytes 4194304 | tf_op jit(solution)/shard_map/while/body/eval_jaxpr/xyhqk,xyqhd->xykhd/transpose | solution.py:135
  66.6 5.4 %concatenate.59 = f32[2,8,16,16,128]{4,3,2,1,0:T(8,128)} reshape(f32[2,8,256,2,64]{4,3,2,1,0:T(2,128)} %copy.45) | data formatting | bytes 4194304 | tf_op jit(solution)/shard_map/while/body/eval_jaxpr/concatenate | solution.py:138
  72.0 1.9 maximum_bitcast_fusion
  75.6 2.9 collective-permute-start.4
  78.5 1.5 collective-permute-start.5
  81.3 4.0 collective-permute-done.5
  85.4 3.6 collective-permute-start.6
  89.0 1.9 collective-permute-start.7
  93.3 1.2 collective-permute-done.7
  99.1 78.2 %psum.23 = f32[128]{0:T(128)S(1)} all-reduce(f32[128]{0:T(128)S(1)} %get-tuple-element.77), channel_id=1, replica_groups=mesh['gx'=32,'gy'=8] {'gx','gy'}, use_global_device_ids=true, to_apply=%region_7.8 | all-reduce | flops 128 | bytes 1024 | tf_op jit(solution)/shard_map/psum | solution.py:238
  178.9 243.5 %all-reduce.8.cloned.1.call-done = (f32[128,384]{1,0:T(8,128)}, f32[128,128]{1,0:T(8,128)}) async-done(((f32[128,384]{1,0:T(8,128)}, f32[128,128]{1,0:T(8,128)}), (f32[128,384]{1,0:T(8,128)}, f32[128,128]{1,0:T(8,128)})) %all-reduce.8.cloned.1.call-update) | async-done | bytes 262160 | tf_op jit(solution)/shard_map/psum | solution.py:238
  422.5 1.6 broadcast_multiply_fusion.1
  424.1 1.5 broadcast_multiply_fusion.2
  (102 shorter events, 19.8 us)
Async XLA Ops:
  7.2 3.2 copy-start
  7.2 415.3 %all-reduce.8.cloned.1.call-start = ((), (), s32[]{:S(2)}) async-start(), calls=%async_computation | async-start | bytes 524288 | tf_op jit(solution)/shard_map/psum | solution.py:238
  9.6 0.7 copy-start.7
  10.7 19.9 %copy-start.2 = (bf16[1,16,64,128]{3,2,1,0:T(8,128)(2,1)S(1)}, bf16[1,16,64,128]{3,2,1,0:T(8,128)(2,1)}, u32[]{:S(2)}) copy-start(bf16[1,16,64,128]{3,2,1,0:T(8,128)(2,1)} %param.17) | copy-start | bytes 786436
  10.7 19.9 %copy-start.15 = (bf16[128,128]{1,0:T(8,128)(2,1)S(1)}, bf16[128,128]{1,0:T(8,128)(2,1)}, u32[]{:S(2)}) copy-start(bf16[128,128]{1,0:T(8,128)(2,1)} %param.16) | copy-start | bytes 98308
  11.5 7.5 %collective-permute-start = (bf16[1,3,64,256]{3,2,1,0:T(8,128)(2,1)}, bf16[1,3,64,256]{3,2,1,0:T(8,128)(2,1)}, u32[]{:S(2)}, u32[]{:S(2)}) collective-permute-start(bf16[1,3,64,256]{3,2,1,0:T(8,128)(2,1)} %get-tuple-element.97), channel_id=1, source_target_pairs={{0,8},{8,16},{16,24},{24,32},{32,40},{40,48},{48,56},{56,64},{64,7... | collective-permute-start | bytes 294920 | tf_op jit(solution)/shard_map/ppermute | solution.py:19
  16.5 5.7 %collective-permute-start.1 = (bf16[1,3,64,256]{3,2,1,0:T(8,128)(2,1)}, bf16[1,3,64,256]{3,2,1,0:T(8,128)(2,1)}, u32[]{:S(2)}, u32[]{:S(2)}) collective-permute-start(bf16[1,3,64,256]{3,2,1,0:T(8,128)(2,1)} %get-tuple-element.98), channel_id=1, source_target_pairs={{8,0},{16,8},{24,16},{32,24},{40,32},{48,40},{56,48},{64,56},{72,6... | collective-permute-start | bytes 294920 | tf_op jit(solution)/shard_map/ppermute | solution.py:20
  18.9 12.7 %copy-start.5 = (bf16[1024,128]{1,0:T(8,128)(2,1)S(1)}, bf16[1024,128]{1,0:T(8,128)(2,1)}, u32[]{:S(2)}) copy-start(bf16[1024,128]{1,0:T(8,128)(2,1)} %fusion.22) | copy-start | bytes 786436
  23.6 8.8 %collective-permute-start.2 = (bf16[1,22,3,256]{3,2,1,0:T(4,128)(2,1)}, bf16[1,22,3,256]{3,2,1,0:T(4,128)(2,1)}, u32[]{:S(2)}, u32[]{:S(2)}) collective-permute-start(bf16[1,22,3,256]{3,2,1,0:T(4,128)(2,1)} %get-tuple-element.95), channel_id=1, source_target_pairs={{0,1},{1,2},{2,3},{3,4},{4,5},{5,6},{6,7},{8,9},{9,10},{10,11},{11... | collective-permute-start | bytes 101384 | tf_op jit(solution)/shard_map/ppermute | solution.py:19
  28.7 5.7 %collective-permute-start.3 = (bf16[1,22,3,256]{3,2,1,0:T(4,128)(2,1)}, bf16[1,22,3,256]{3,2,1,0:T(4,128)(2,1)}, u32[]{:S(2)}, u32[]{:S(2)}) collective-permute-start(bf16[1,22,3,256]{3,2,1,0:T(4,128)(2,1)} %get-tuple-element.96), channel_id=1, source_target_pairs={{1,0},{2,1},{3,2},{4,3},{5,4},{6,5},{7,6},{9,8},{10,9},{11,10},{12... | collective-permute-start | bytes 101384 | tf_op jit(solution)/shard_map/ppermute | solution.py:20
  42.1 1.2 copy-start.6
  75.4 4.7 %copy-start.1 = (bf16[1,16,64,128]{3,2,1,0:T(8,128)(2,1)S(1)}, bf16[1,16,64,128]{3,2,1,0:T(8,128)(2,1)}, u32[]{:S(2)}) copy-start(bf16[1,16,64,128]{3,2,1,0:T(8,128)(2,1)} %param.13) | copy-start | bytes 786436
  75.4 4.7 %copy-start.16 = (bf16[128,128]{1,0:T(8,128)(2,1)S(1)}, bf16[128,128]{1,0:T(8,128)(2,1)}, u32[]{:S(2)}) copy-start(bf16[128,128]{1,0:T(8,128)(2,1)} %param.16) | copy-start | bytes 98308
  75.5 15.4 %copy-start.3 = (bf16[1,16,64,128]{3,2,1,0:T(8,128)(2,1)S(1)}, bf16[1,16,64,128]{3,2,1,0:T(8,128)(2,1)}, u32[]{:S(2)}) copy-start(bf16[1,16,64,128]{3,2,1,0:T(8,128)(2,1)} %param.17) | copy-start | bytes 786436
  75.6 5.7 %collective-permute-start.4 = (bf16[1,3,70,256]{3,2,1,0:T(8,128)(2,1)S(1)}, bf16[1,3,70,256]{3,2,1,0:T(8,128)(2,1)S(1)}, u32[]{:S(2)}, u32[]{:S(2)}) collective-permute-start(bf16[1,3,70,256]{3,2,1,0:T(8,128)(2,1)S(1)} %get-tuple-element.91), channel_id=1, source_target_pairs={{0,8},{8,16},{16,24},{24,32},{32,40},{40,48},{48,56},{56,64},{64,7... | collective-permute-start | bytes 322568 | tf_op jit(solution)/shard_map/ppermute | solution.py:19
  78.5 6.8 %collective-permute-start.5 = (bf16[1,3,70,256]{3,2,1,0:T(8,128)(2,1)S(1)}, bf16[1,3,70,256]{3,2,1,0:T(8,128)(2,1)S(1)}, u32[]{:S(2)}, u32[]{:S(2)}) collective-permute-start(bf16[1,3,70,256]{3,2,1,0:T(8,128)(2,1)S(1)} %get-tuple-element.92), channel_id=1, source_target_pairs={{8,0},{16,8},{24,16},{32,24},{40,32},{48,40},{56,48},{64,56},{72,6... | collective-permute-start | bytes 322568 | tf_op jit(solution)/shard_map/ppermute | solution.py:20
  85.4 8.0 %collective-permute-start.6 = (bf16[1,28,3,256]{3,2,1,0:T(4,128)(2,1)S(1)}, bf16[1,28,3,256]{3,2,1,0:T(4,128)(2,1)S(1)}, u32[]{:S(2)}, u32[]{:S(2)}) collective-permute-start(bf16[1,28,3,256]{3,2,1,0:T(4,128)(2,1)S(1)} %get-tuple-element.89), channel_id=1, source_target_pairs={{0,1},{1,2},{2,3},{3,4},{4,5},{5,6},{6,7},{8,9},{9,10},{10,11},{11... | collective-permute-start | bytes 129032 | tf_op jit(solution)/shard_map/ppermute | solution.py:19
  89.0 5.5 %collective-permute-start.7 = (bf16[1,28,3,256]{3,2,1,0:T(4,128)(2,1)S(1)}, bf16[1,28,3,256]{3,2,1,0:T(4,128)(2,1)S(1)}, u32[]{:S(2)}, u32[]{:S(2)}) collective-permute-start(bf16[1,28,3,256]{3,2,1,0:T(4,128)(2,1)S(1)} %get-tuple-element.90), channel_id=1, source_target_pairs={{1,0},{2,1},{3,2},{4,3},{5,4},{6,5},{7,6},{9,8},{10,9},{11,10},{12... | collective-permute-start | bytes 129032 | tf_op jit(solution)/shard_map/ppermute | solution.py:20
  93.3 1.2 copy-start.9
  94.5 0.6 copy-start.11
  95.5 0.8 copy-start.10
  95.6 0.8 copy-start.12
  96.6 1.0 copy-start.8
  96.6 1.0 copy-start.13
  96.7 1.9 copy-start.17
  97.0 1.6 copy-start.14
  97.6 79.8 %copy-start.4 = (bf16[1,16,64,128]{3,2,1,0:T(8,128)(2,1)S(1)}, bf16[1,16,64,128]{3,2,1,0:T(8,128)(2,1)}, u32[]{:S(2)}) copy-start(bf16[1,16,64,128]{3,2,1,0:T(8,128)(2,1)} %param.17) | copy-start | bytes 786436
Sparse Core Ops, SparseCore 0:
  177.5 244.9 all-reduce.7
where the time goes:
time: 434 us; the launch traced here: 432 us
  waiting for transfers between devices  254 us (59%)
  blocking collectives  78.2 us (18%)
  local copies, waits for them, and re-layouts  37.1 us (9%)
  starting transfers between devices  23.3 us (5%)
  other arithmetic  15.1 us (3%)
  between operations  14.7 us (3%)
  matrix products  10.2 us (2%)
    psum x1, waiting for transfers between devices, per_device(): lax.psum((local_qkv, local_output, local_gain), ('gx', 'gy'))  244 us
    psum x1, blocking collectives, per_device(): lax.psum((local_qkv, local_output, local_gain), ('gx', 'gy'))  78.2 us
    ppermute x4, starting transfers between devices, padded_2(): before = lax.ppermute(last, axis, up)  16.7 us
    ppermute x4, waiting for transfers between devices, padded_2(): after = lax.ppermute(first, axis, down)  10.4 us
    concatenate x2, local copies, waits for them, and re-layouts, query_side(): jnp.concatenate([d_key.reshape(block_rows, block_cols, 256, channels), d_...  9.69 us
  transfers between devices with their start and end apart: 9, of which 5 were waited for; matrix products, arithmetic and copies ran while one was open for 2% of the time, Pallas kernels for 0%

commit v1 on v0

v1 whole, which is shorter than its diff:
```python
import functools

import jax
import jax.numpy as jnp
from jax import lax
from jax.experimental import pallas as pl
from jax.experimental.pallas import tpu as pltpu
from jax.sharding import PartitionSpec as P

MESH = pl.DeviceIdType.MESH
EPS = 1e-06
F32 = jnp.float32
BF16 = jnp.bfloat16
C = 128
RL, CL = 16, 64
RE, CE = RL + 6, CL + 8
NB = CL // 8
KEYS = RE * 16
NEG = -1e30
ZN = 8

NT = (((1,), (1,)), ((), ()))
TN = (((0,), (0,)), ((), ()))


def dot(a, b, dims=(((1,), (0,)), ((), ()))):
    return lax.dot_general(a, b, dims, preferred_element_type=F32)


def inverse_rms(x):
    return lax.rsqrt(jnp.sum(x * x, axis=-1, keepdims=True) * (1.0 / C) + EPS)


def kernel(
    gxn, gyn, zn,
    tok, gain, wqkv, wout, cot,
    out, tgrad, qkvg, outg, gaing,
    rx_rows, rx_cols, rx_corner,
    x_ext, u_ext, k_ext, v_ext, dk_ext, dv_ext,
    q2, da2, att, dq, near,
    tx2_rows, tx2_cols, tx2_corner, rx2_rows, rx2_cols, rx2_corner,
    gsum, g16, rs_rx, z_rx, ag,
    h_send, h_recv, d_send, d_recv, a_send, a_recv,
):
    yn = gxn // zn
    na = yn * gyn
    rows = 512 // na
    gx = lax.axis_index("gx")
    gy = lax.axis_index("gy")
    y, z = gx // zn, gx % zn
    me = y * gyn + gy

    def beside(dr, dc):
        return ((gx + dr + gxn) % gxn, (gy + dc + gyn) % gyn)

    def plane(d):
        m = (me + d) % na
        return m, ((m // gyn) * zn + z, m % gyn)

    def column(d):
        return (y * zn + (z + d) % zn, gy)

    around = [(dr, dc) for dr in (-1, 0, 1) for dc in (-1, 0, 1) if dr or dc]
    barrier = pltpu.get_barrier_semaphore()
    for dr, dc in around:
        pl.semaphore_signal(barrier, inc=1, device_id=beside(dr, dc), device_id_type=MESH)
    for d in range(1, zn):
        pl.semaphore_signal(barrier, inc=1, device_id=column(d), device_id_type=MESH)
    for d in range(1, na):
        pl.semaphore_signal(barrier, inc=1, device_id=plane(d)[1], device_id_type=MESH)

    lane = lax.broadcasted_iota(jnp.int32, (1, C), 1)
    head0 = lane < 64

    def two_heads(v):
        v = v.astype(BF16)
        zero = jnp.zeros_like(v)
        return jnp.concatenate([jnp.where(head0, v, zero), jnp.where(head0, zero, v)], axis=0)

    x = tok[...].astype(F32).reshape(RL * CL, C)
    x_ext[3 : RL + 3, 4 : CL + 4, :] = x.reshape(RL, CL, C)
    unit = x * inverse_rms(x)
    normed = (unit * gain[...]).astype(BF16)
    query = (dot(normed, wqkv[:, 0:C]) * 0.125).reshape(RL, CL, C)
    d_att = dot(cot[...].reshape(RL * CL, C), wout[...], NT).reshape(RL, CL, C)
    for j in range(NB):
        q2[j] = two_heads(query[:, 8 * j : 8 * j + 8, :].reshape(RL * 8, C))
        da2[j] = two_heads(d_att[:, 8 * j : 8 * j + 8, :].reshape(RL * 8, C))

    key_at = lax.broadcasted_iota(jnp.int32, (RE, 16, 256), 0)
    key_col = lax.broadcasted_iota(jnp.int32, (RE, 16, 256), 1)
    at = lax.broadcasted_iota(jnp.int32, (RE, 16, 256), 2)
    q_row = (at // 8) % RL
    q_col = at % 8
    image_row = gx * RL + key_at - 3
    ok = (
        (key_at >= q_row) & (key_at <= q_row + 6)
        & (key_col >= q_col + 1) & (key_col <= q_col + 7)
        & (image_row >= 0) & (image_row < gxn * RL)
    )
    near[...] = jnp.where(ok, 0.0, NEG)
    dk_ext[...] = jnp.zeros_like(dk_ext)
    dv_ext[...] = jnp.zeros_like(dv_ext)

    pl.semaphore_wait(barrier, 8 + (zn - 1) + (na - 1))

    copies = []
    for i, (dr, dc) in enumerate(around):
        rsl = slice(0, RL) if dr == 0 else (slice(0, 3) if dr < 0 else slice(RL - 3, RL))
        csl = slice(0, CL) if dc == 0 else (slice(0, 16) if dc < 0 else slice(CL - 16, CL))
        src = tok.at[rsl, csl]
        if dc == 0:
            dst = rx_rows.at[0 if dr > 0 else 1]
        elif dr == 0:
            dst = rx_cols.at[0 if dc > 0 else 1]
        else:
            dst = rx_corner.at[(0 if dr > 0 else 2) + (0 if dc > 0 else 1)]
        copy = pltpu.make_async_remote_copy(
            src, dst, h_send.at[i], h_recv.at[i], device_id=beside(dr, dc), device_id_type=MESH
        )
        copy.start()
        copies.append(copy)
    for copy in copies:
        copy.wait()

    x_ext[0:3, 4 : CL + 4, :] = rx_rows[0].astype(F32)
    x_ext[RL + 3 : RE, 4 : CL + 4, :] = rx_rows[1].astype(F32)
    x_ext[3 : RL + 3, 0:4, :] = rx_cols[0].astype(F32)[:, 12:16]
    x_ext[3 : RL + 3, CL + 4 : CE, :] = rx_cols[1].astype(F32)[:, 0:4]
    x_ext[0:3, 0:4, :] = rx_corner[0].astype(F32)[:, 12:16]
    x_ext[0:3, CL + 4 : CE, :] = rx_corner[1].astype(F32)[:, 0:4]
    x_ext[RL + 3 : RE, 0:4, :] = rx_corner[2].astype(F32)[:, 12:16]
    x_ext[RL + 3 : RE, CL + 4 : CE, :] = rx_corner[3].astype(F32)[:, 0:4]
    xe = x_ext[...].reshape(RE * CE, C)
    ue = xe * inverse_rms(xe)
    u_ext[...] = ue.astype(BF16)
    keyval = dot((ue * gain[...]).astype(BF16), wqkv[:, C : 3 * C])
    k_ext[...] = keyval[:, 0:C].reshape(RE, CE, C)
    v_ext[...] = keyval[:, C : 2 * C].reshape(RE, CE, C)

    def block(j, carry):
        j0 = pl.multiple_of(j * 8, 8)
        window = pl.ds(j0, 16)
        kw = k_ext[:, window, :].reshape(KEYS, C).astype(BF16)
        vw = v_ext[:, window, :].reshape(KEYS, C).astype(BF16)
        qb, db = q2[j], da2[j]
        scores = dot(kw, qb, NT).reshape(RE, 16, 256)
        image_col = gy * CL + j0 - 4 + lax.broadcasted_iota(jnp.int32, (1, 16, 256), 1)
        edge = jnp.where((image_col >= 0) & (image_col < gyn * CL), 0.0, NEG)
        weights = jnp.exp(scores + near[...] + edge).reshape(KEYS, 256)
        totals = jnp.sum(weights, axis=0, keepdims=True)
        shares = weights * (1.0 / totals)
        shares_low = shares.astype(BF16)
        d_shares = dot(vw, db, NT)
        delta = jnp.sum(shares * d_shares, axis=0, keepdims=True)
        d_scores = (shares * (d_shares - delta)).astype(BF16)
        a2 = dot(shares_low, vw, TN)
        dq2 = dot(d_scores, kw, TN)
        own = pl.ds(j0, 8)
        att[:, own, :] = jnp.where(head0, a2[0:128], a2[128:256]).reshape(RL, 8, C)
        dq[:, own, :] = jnp.where(head0, dq2[0:128], dq2[128:256]).reshape(RL, 8, C)
        dk_ext[:, window, :] += dot(d_scores, qb).reshape(RE, 16, C)
        dv_ext[:, window, :] += dot(shares_low, db).reshape(RE, 16, C)
        return carry

    lax.fori_loop(0, NB, block, 0)

    attended = att[...].reshape(RL * CL, C).astype(BF16)
    d_query = (dq[...] * 0.125).reshape(RL * CL, C).astype(BF16)
    cot_rows = cot[...].reshape(RL * CL, C)
    u = u_ext[...]
    gsum[0:C, :] = dot(unit.astype(BF16), d_query, TN)
    gsum[C : 2 * C, :] = dot(u, dk_ext[...].reshape(RE * CE, C).astype(BF16), TN)
    gsum[2 * C : 3 * C, :] = dot(u, dv_ext[...].reshape(RE * CE, C).astype(BF16), TN)
    gsum[3 * C : 4 * C, :] = dot(attended, cot_rows, TN)
    g16[...] = gsum[...].astype(BF16)
    for d in range(1, na):
        m, device = plane(d)
        pltpu.make_async_remote_copy(
            g16.at[pl.ds(pl.multiple_of(m * rows, rows), rows)],
            rs_rx.at[pl.ds((d - 1) * rows, rows)],
            a_send.at[0], a_recv.at[0], device_id=device, device_id_type=MESH,
        ).start()

    both = jnp.concatenate([dk_ext[...], dv_ext[...]], axis=-1)
    pad_rows = jnp.zeros((8, 2 * C), F32)
    for i, lo in enumerate((0, RL + 3)):
        flat = both[lo : lo + 3].reshape(3 * CE, 2 * C)
        tx2_rows[i] = jnp.concatenate([flat, pad_rows], axis=0).astype(BF16)
        for k, left in enumerate((0, CL)):
            corner = both[lo : lo + 3, left : left + 8].reshape(24, 2 * C)
            tx2_corner[2 * i + k] = jnp.concatenate([corner, pad_rows], axis=0).astype(BF16)
    for k, left in enumerate((0, CL)):
        tx2_cols[k] = both[3 : RL + 3, left : left + 8].reshape(RL * 8, 2 * C).astype(BF16)
    back = []
    for i, (dr, dc) in enumerate(around):
        if dc == 0:
            n = 0 if dr < 0 else 1
            src, dst = tx2_rows.at[n], rx2_rows.at[n]
        elif dr == 0:
            n = 0 if dc < 0 else 1
            src, dst = tx2_cols.at[n], rx2_cols.at[n]
        else:
            n = (0 if dr < 0 else 2) + (0 if dc < 0 else 1)
            src, dst = tx2_corner.at[n], rx2_corner.at[n]
        copy = pltpu.make_async_remote_copy(
            src, dst, d_send.at[i], d_recv.at[i], device_id=beside(dr, dc), device_id_type=MESH
        )
        copy.start()
        back.append(copy)

    out[...] = (x + dot(attended, wout[...])).astype(BF16).reshape(RL, CL, C)

    def wait_bytes(ref, sem):
        pltpu.make_async_copy(ref, ref, sem).wait()

    wait_bytes(rs_rx, a_recv.at[0])
    mine = gsum[pl.ds(pl.multiple_of(me * rows, rows), rows), :]
    parts = rs_rx[...].astype(F32).reshape(na - 1, rows, C)
    z_rx[pl.ds(z, 1)] = (mine + jnp.sum(parts, axis=0)).astype(BF16)[None]
    for d in range(1, zn):
        pltpu.make_async_remote_copy(
            z_rx.at[z], z_rx.at[z],
            a_send.at[1], a_recv.at[1], device_id=column(d), device_id_type=MESH,
        ).start()

    for copy in back:
        copy.wait()
    sub = lax.broadcasted_iota(jnp.int32, (1, 8, 1), 1)
    tile = lax.broadcasted_iota(jnp.int32, (1, CE, 1), 1)
    inner = (tile >= 4) & (tile < CL + 4)

    def add(rsl, csl, rx, n, mask):
        shape = (rsl.stop - rsl.start, csl.stop - csl.start, 2 * C)
        add_rows = rx[n].astype(F32)[0 : shape[0] * shape[1]].reshape(shape)
        add_rows = jnp.where(mask, add_rows, 0.0)
        dk_ext[rsl, csl, :] += add_rows[:, :, 0:C]
        dv_ext[rsl, csl, :] += add_rows[:, :, C : 2 * C]

    first, last = slice(3, 6), slice(RL, RL + 3)
    left, right = slice(0, 8), slice(CL, CE)
    add(last, slice(0, CE), rx2_rows, 0, inner)
    add(first, slice(0, CE), rx2_rows, 1, inner)
    add(slice(3, RL + 3), right, rx2_cols, 0, sub < 4)
    add(slice(3, RL + 3), left, rx2_cols, 1, sub >= 4)
    add(last, right, rx2_corner, 0, sub < 4)
    add(last, left, rx2_corner, 1, sub >= 4)
    add(first, right, rx2_corner, 2, sub < 4)
    add(first, left, rx2_corner, 3, sub >= 4)
    d_key = dk_ext[3 : RL + 3, 4 : CL + 4, :].reshape(RL * CL, C).astype(BF16)
    d_value = dv_ext[3 : RL + 3, 4 : CL + 4, :].reshape(RL * CL, C).astype(BF16)
    d_normed = (
        dot(d_query, wqkv[:, 0:C], NT)
        + dot(d_key, wqkv[:, C : 2 * C], NT)
        + dot(d_value, wqkv[:, 2 * C : 3 * C], NT)
    )
    x = tok[...].astype(F32).reshape(RL * CL, C)
    r = inverse_rms(x)
    unit = x * r
    g = d_normed * gain[...]
    mean = jnp.sum(g * unit, axis=-1, keepdims=True) * (1.0 / C)
    grads = cot_rows.astype(F32) + r * (g - unit * mean)
    tgrad[...] = grads.astype(BF16).reshape(RL, CL, C)

    wait_bytes(z_rx.at[pl.ds(0, zn - 1)], a_recv.at[1])
    wait_bytes(z_rx.at[pl.ds(0, zn - 1)], a_send.at[1])
    here = pl.ds(pl.multiple_of(me * rows, rows), rows)
    ag[here, :] = jnp.sum(z_rx[...].astype(F32), axis=0).astype(BF16)
    for d in range(1, na):
        m, device = plane(d)
        pltpu.make_async_remote_copy(
            ag.at[here], ag.at[here],
            a_send.at[2], a_recv.at[2], device_id=device, device_id_type=MESH,
        ).start()
    wait_bytes(rs_rx, a_send.at[0])
    wait_bytes(rs_rx, a_recv.at[2])
    wait_bytes(rs_rx, a_send.at[2])
    factor = (gxn * RL * gyn * CL) ** (-0.5)
    eye = lax.broadcasted_iota(jnp.int32, (C, C), 0) == lax.broadcasted_iota(jnp.int32, (C, C), 1)
    gain_col = jnp.sum(jnp.where(eye, gain[...], 0.0), axis=1, keepdims=True)
    total = jnp.zeros((C, C), F32)
    for i in range(3):
        piece = ag[i * C : (i + 1) * C, :].astype(F32) * factor
        qkvg[:, i * C : (i + 1) * C] = piece * gain_col
        total += piece * wqkv[:, i * C : (i + 1) * C].astype(F32)
    outg[...] = ag[3 * C : 4 * C, :].astype(F32) * factor
    gain_sum = jnp.sum(total, axis=1, keepdims=True)
    gaing[...] = jnp.sum(jnp.where(eye, gain_sum, 0.0), axis=0, keepdims=True)


def per_device(gxn, gyn, zn, tokens, norm_gain, qkv_weight, output_weight, cotangent):
    na = (gxn // zn) * gyn
    rows = 512 // na
    vmem = pl.BlockSpec(memory_space=pltpu.VMEM)
    sds = jax.ShapeDtypeStruct
    outs = pl.pallas_call(
        functools.partial(kernel, gxn, gyn, zn),
        out_shape=(
            sds((RL, CL, C), BF16),
            sds((RL, CL, C), BF16),
            sds((C, 3 * C), F32),
            sds((C, C), F32),
            sds((1, C), F32),
        ),
        in_specs=[vmem] * 5,
        out_specs=(vmem,) * 5,
        scratch_shapes=[
            pltpu.VMEM((2, 3, CL, C), BF16),
            pltpu.VMEM((2, RL, 16, C), BF16),
            pltpu.VMEM((4, 3, 16, C), BF16),
            pltpu.VMEM((RE, CE, C), F32),
            pltpu.VMEM((RE * CE, C), BF16),
            pltpu.VMEM((RE, CE, C), F32),
            pltpu.VMEM((RE, CE, C), F32),
            pltpu.VMEM((RE, CE, C), F32),
            pltpu.VMEM((RE, CE, C), F32),
            pltpu.VMEM((NB, 256, C), BF16),
            pltpu.VMEM((NB, 256, C), BF16),
            pltpu.VMEM((RL, CL, C), F32),
            pltpu.VMEM((RL, CL, C), F32),
            pltpu.VMEM((RE, 16, 256), F32),
            pltpu.VMEM((2, 224, 2 * C), BF16),
            pltpu.VMEM((2, RL * 8, 2 * C), BF16),
            pltpu.VMEM((4, 32, 2 * C), BF16),
            pltpu.VMEM((2, 224, 2 * C), BF16),
            pltpu.VMEM((2, RL * 8, 2 * C), BF16),
            pltpu.VMEM((4, 32, 2 * C), BF16),
            pltpu.VMEM((4 * C, C), F32),
            pltpu.VMEM((4 * C, C), BF16),
            pltpu.VMEM(((na - 1) * rows, C), BF16),
            pltpu.VMEM((zn, rows, C), BF16),
            pltpu.VMEM((4 * C, C), BF16),
            pltpu.SemaphoreType.DMA((8,)),
            pltpu.SemaphoreType.DMA((8,)),
            pltpu.SemaphoreType.DMA((8,)),
            pltpu.SemaphoreType.DMA((8,)),
            pltpu.SemaphoreType.DMA((3,)),
            pltpu.SemaphoreType.DMA((3,)),
        ],
        compiler_params=pltpu.CompilerParams(
            collective_id=0, has_side_effects=True, vmem_limit_bytes=40 << 20
        ),
    )(
        tokens.reshape(RL, CL, C),
        norm_gain.reshape(1, C),
        qkv_weight,
        output_weight,
        cotangent.reshape(RL, CL, C),
    )
    out, tgrad, qkvg, outg, gaing = outs
    return (
        out.reshape(tokens.shape),
        tgrad.reshape(tokens.shape),
        qkvg,
        outg,
        gaing.reshape(C),
    )


def solution(mesh):
    gxn, gyn = mesh.shape["gx"], mesh.shape["gy"]
    image = P(None, "gx", "gy", None)
    return jax.shard_map(
        functools.partial(per_device, gxn, gyn, min(ZN, max(gxn // 4, 2))),
        mesh=mesh,
        in_specs=(image, P(), P(), P(), image),
        out_specs=(image, image, P(), P(), P()),
        check_vma=False,
    )
```

time: 434 us -> 46.8 us (0.11)
  waiting for transfers between devices: 254 us -> 0 us
  blocking collectives: 78.2 us -> 0 us
  Pallas kernels: 0 us -> 38.5 us
  local copies, waits for them, and re-layouts: 37.1 us -> 7.42 us
  starting transfers between devices: 23.3 us -> 0 us
  other arithmetic: 15.1 us -> 0 us
  between operations: 14.7 us -> 0.66 us
  matrix products: 10.2 us -> 0 us
    psum x1 -> x0, waiting for transfers between devices: 244 us -> none  [per_device(): lax.psum((local_qkv, local_output, local_gain), ('gx', 'gy'))]
    psum x1 -> x0, blocking collectives: 78.2 us -> none  [per_device(): lax.psum((local_qkv, local_output, local_gain), ('gx', 'gy'))]
    pallas_call x0 -> x1, Pallas kernels: none -> 38.5 us  [per_device(): pl.pallas_call(functools.partial(kernel, gxn, gyn, zn), out_shape=(sds((R...]
    ppermute x8 -> x0, starting transfers between devices: 23.3 us -> none  [the longest x4 16.7 us: padded_2(): before = lax.ppermute(last, axis, up)]
    transpose x3 -> x0, local copies, waits for them, and re-layouts: 11.3 us -> none  [the longest x1 6.68 us: query_side(): jnp.einsum('xyhqk,xyqhd->xykhd', shares_low, grad_blocks, preferred_eleme...]
    ppermute x8 -> x0, waiting for transfers between devices: 10.4 us -> none  [the longest x4 10.4 us: padded_2(): after = lax.ppermute(first, axis, down)]
    dot_general x12 -> x0, matrix products: 10.2 us -> none  [the longest x1 2.03 us: query_side(): jnp.einsum('xyhqk,xyqhd->xykhd', shares_low, grad_blocks, preferred_eleme...]
    concatenate x2 -> x0, local copies, waits for them, and re-layouts: 9.69 us -> none  [query_side(): jnp.concatenate([d_key.reshape(block_rows, block_cols, 256, channels), d_...]
  transfers between devices with their start and end apart: 9 -> 0, of which waited for: 5 -> 0; matrix products, arithmetic and copies ran while one was open for 2% -> 0% of each run, Pallas kernels for 0% -> 0%
where the time goes in v1:
time: 46.8 us; the launch traced here: 46.6 us
  Pallas kernels  38.5 us (82%)
  local copies, waits for them, and re-layouts  7.42 us (16%)
  between operations  0.66 us (1%)
    pallas_call x1, Pallas kernels, per_device(): pl.pallas_call(functools.partial(kernel, gxn, gyn, zn), out_shape=(sds((R...  38.5 us
    unnamed x15, local copies, waits for them, and re-layouts  7.42 us

profile of v1, /device:TPU:1, one launch (start us, length us, event | category | flops | bytes accessed | tf_op | source)
XLA Modules:
  0.0 46.6 jit_solution(4300554728449028164)
XLA Ops:
  0.6 0.0 copy-start.4
  0.6 0.6 %copy-done.4 = f32[128]{0:T(128)S(1)} copy-done((f32[128]{0:T(128)S(1)}, f32[128]{0:T(128)}, u32[]{:S(2)}) %copy-start.4) | copy-done | bytes 536
  1.3 0.0 copy-start
  1.3 0.9 %copy-done = bf16[1,16,64,128]{3,2,1,0:T(8,128)(2,1)S(1)} copy-done((bf16[1,16,64,128]{3,2,1,0:T(8,128)(2,1)S(1)}, bf16[1,16,64,128]{3,2,1,0:T(8,128)(2,1)}, u32[]{:S(2)}) %copy-start) | copy-done | bytes 262168
  2.2 0.0 copy-start.1
  2.2 0.9 %copy-done.1 = bf16[1,16,64,128]{3,2,1,0:T(8,128)(2,1)S(1)} copy-done((bf16[1,16,64,128]{3,2,1,0:T(8,128)(2,1)S(1)}, bf16[1,16,64,128]{3,2,1,0:T(8,128)(2,1)}, u32[]{:S(2)}) %copy-start.1) | copy-done | bytes 262168
  3.2 0.0 copy-start.2
  3.2 0.9 %copy-done.2 = bf16[128,384]{1,0:T(8,128)(2,1)S(1)} copy-done((bf16[128,384]{1,0:T(8,128)(2,1)S(1)}, bf16[128,384]{1,0:T(8,128)(2,1)}, u32[]{:S(2)}) %copy-start.2) | copy-done | bytes 98328
  4.1 0.0 copy-start.3
  4.1 0.8 %copy-done.3 = bf16[128,128]{1,0:T(8,128)(2,1)S(1)} copy-done((bf16[128,128]{1,0:T(8,128)(2,1)S(1)}, bf16[128,128]{1,0:T(8,128)(2,1)}, u32[]{:S(2)}) %copy-start.3) | copy-done | bytes 32792
  4.8 38.5 %shard_map.92 = (bf16[16,64,128]{2,1,0:T(8,128)(2,1)S(1)}, bf16[16,64,128]{2,1,0:T(8,128)(2,1)S(1)}, f32[128,384]{1,0:T(8,128)S(1)}, f32[128,128]{1,0:T(8,128)S(1)}, f32[1,128]{1,0:T(1,128)S(1)}) custom-call(bf16[16,64,128]{2,1,0:T(8,128)(2,1)S(1)} %bitcast.6, f32[1,128]{1,0:T(1,128)S(1)} %bitcast.10, bf16[128,384]{1,0:T(8,128)(2,1)S(1)} %copy-done.2, ...), custom_call_target="tpu_custom_call" | custom-call | tf_op jit(solution)/shard_map/pallas_call | solution.py:296
  43.4 0.7 %copy.15 = bf16[1,16,64,128]{3,2,1,0:T(8,128)(2,1)} copy(bf16[1,16,64,128]{3,2,1,0:T(8,128)(2,1)S(1)} %bitcast.9) | data formatting | bytes 524288
  44.1 0.7 %copy.16 = bf16[1,16,64,128]{3,2,1,0:T(8,128)(2,1)} copy(bf16[1,16,64,128]{3,2,1,0:T(8,128)(2,1)S(1)} %bitcast.8) | data formatting | bytes 524288
  44.8 0.7 %copy.17 = f32[128,384]{1,0:T(8,128)} copy(f32[128,384]{1,0:T(8,128)S(1)} %get-tuple-element.22) | data formatting | bytes 393216
  45.4 0.6 %copy.18 = f32[128,128]{1,0:T(8,128)} copy(f32[128,128]{1,0:T(8,128)S(1)} %get-tuple-element.23) | data formatting | bytes 131072
  46.1 0.5 %copy.19 = f32[128]{0:T(128)} copy(f32[128]{0:T(128)S(1)} %bitcast.11) | data formatting | bytes 1024
Async XLA Ops:
  0.6 0.7 %copy-start.4 = (f32[128]{0:T(128)S(1)}, f32[128]{0:T(128)}, u32[]{:S(2)}) copy-start(f32[128]{0:T(128)} %param.6) | copy-start | bytes 1540
  1.3 0.9 %copy-start = (bf16[1,16,64,128]{3,2,1,0:T(8,128)(2,1)S(1)}, bf16[1,16,64,128]{3,2,1,0:T(8,128)(2,1)}, u32[]{:S(2)}) copy-start(bf16[1,16,64,128]{3,2,1,0:T(8,128)(2,1)} %param.5) | copy-start | bytes 786436
  2.2 0.9 %copy-start.1 = (bf16[1,16,64,128]{3,2,1,0:T(8,128)(2,1)S(1)}, bf16[1,16,64,128]{3,2,1,0:T(8,128)(2,1)}, u32[]{:S(2)}) copy-start(bf16[1,16,64,128]{3,2,1,0:T(8,128)(2,1)} %param.9) | copy-start | bytes 786436
  3.2 0.9 %copy-start.2 = (bf16[128,384]{1,0:T(8,128)(2,1)S(1)}, bf16[128,384]{1,0:T(8,128)(2,1)}, u32[]{:S(2)}) copy-start(bf16[128,384]{1,0:T(8,128)(2,1)} %wqkv.1) | copy-start | bytes 294916
  4.1 0.8 %copy-start.3 = (bf16[128,128]{1,0:T(8,128)(2,1)S(1)}, bf16[128,128]{1,0:T(8,128)(2,1)}, u32[]{:S(2)}) copy-start(bf16[128,128]{1,0:T(8,128)(2,1)} %wout.1) | copy-start | bytes 98308

commit v2 on v1

v2 whole, which is shorter than its diff:
```python
import functools

import jax
import jax.numpy as jnp
from jax import lax
from jax.experimental import pallas as pl
from jax.experimental.pallas import tpu as pltpu
from jax.sharding import PartitionSpec as P

MESH = pl.DeviceIdType.MESH
EPS = 1e-06
F32 = jnp.float32
BF16 = jnp.bfloat16
C = 128
RL, CL = 16, 64
RE, CE = RL + 6, CL + 8
NB = CL // 8
STRIP = 32
INNER_UNROLL = 6
STRIP_UNROLL = 2
NEG = -1e30
ZN = 8

NT = (((1,), (1,)), ((), ()))
TN = (((0,), (0,)), ((), ()))


def dot(a, b, dims=(((1,), (0,)), ((), ()))):
    return lax.dot_general(a, b, dims, preferred_element_type=F32)


def inverse_rms(x):
    return lax.rsqrt(jnp.sum(x * x, axis=-1, keepdims=True) * (1.0 / C) + EPS)


def kernel(
    gxn, gyn, zn,
    tok_hbm, gain_hbm, wqkv_hbm, wout_hbm, cot_hbm,
    out_hbm, tgrad_hbm, qkvg_hbm, outg_hbm, gaing_hbm,
    tok, gain, wqkv, wout, cot,
    out, tgrad, qkvg, outg, gaing,
    rx_rows, rx_cols, rx_corner,
    u_ext, k_ext, v_ext, dk_ext, dv_ext, dn_ext,
    q_loc, da_loc, att, dq,
    tx2_rows, tx2_cols, tx2_corner, rx2_rows, rx2_cols, rx2_corner,
    gsum, g16, rs_rx, z_rx, ag,
    in_sem, out_sem, h_send, h_recv, d_send, d_recv, a_send, a_recv,
):
    yn = gxn // zn
    na = yn * gyn
    rows = 512 // na
    gx = lax.axis_index("gx")
    gy = lax.axis_index("gy")
    y, z = gx // zn, gx % zn
    me = y * gyn + gy

    def beside(dr, dc):
        return ((gx + dr + gxn) % gxn, (gy + dc + gyn) % gyn)

    def exists(dr, dc):
        r, c = gx + dr, gy + dc
        return (r >= 0) & (r < gxn) & (c >= 0) & (c < gyn)

    def plane(d):
        m = (me + d) % na
        return m, ((m // gyn) * zn + z, m % gyn)

    def column(d):
        return (y * zn + (z + d) % zn, gy)

    def wait_bytes(ref, sem):
        pltpu.make_async_copy(ref, ref, sem).wait()

    around = [(dr, dc) for dr in (-1, 0, 1) for dc in (-1, 0, 1) if dr or dc]
    barrier = pltpu.get_barrier_semaphore()

    def greet(device):
        pl.semaphore_signal(barrier, inc=1, device_id=device, device_id_type=MESH)

    for dr, dc in around:
        if dr:
            greet(beside(dr, dc))
    for d in range(1, zn):
        greet(column(d))
    for d in range(1, na):
        greet(plane(d)[1])

    fetches = [
        pltpu.make_async_copy(src, dst, in_sem.at[i])
        for i, (src, dst) in enumerate(
            ((tok_hbm, tok), (gain_hbm, gain), (wqkv_hbm, wqkv), (cot_hbm, cot), (wout_hbm, wout))
        )
    ]
    for fetch in fetches:
        fetch.start()

    pl.semaphore_wait(barrier, 6 + (zn - 1) + (na - 1))

    halo = []
    for i, (dr, dc) in enumerate(around):
        rsl = slice(0, RL) if dr == 0 else (slice(0, 3) if dr < 0 else slice(RL - 3, RL))
        csl = slice(0, CL) if dc == 0 else (slice(0, 16) if dc < 0 else slice(CL - 16, CL))
        src = tok_hbm.at[rsl, csl]
        if dc == 0:
            dst = rx_rows.at[0 if dr > 0 else 1]
        elif dr == 0:
            dst = rx_cols.at[0 if dc > 0 else 1]
        else:
            dst = rx_corner.at[(0 if dr > 0 else 2) + (0 if dc > 0 else 1)]
        copy = pltpu.make_async_remote_copy(
            src, dst, h_send.at[i], h_recv.at[i], device_id=beside(dr, dc), device_id_type=MESH
        )
        halo.append((copy, dst, exists(dr, dc), exists(-dr, -dc)))
    for copy, dst, to, _ in halo:
        pl.when(to)(copy.start)

    for fetch in fetches:
        fetch.wait()
    dk_ext[...] = jnp.zeros_like(dk_ext)
    dv_ext[...] = jnp.zeros_like(dv_ext)
    u_ext[...] = jnp.zeros_like(u_ext)
    gains = gain[...]

    def keyval(unit):
        return dot((unit * gains).astype(BF16), wqkv[:, C : 3 * C])

    x = tok[...].astype(F32).reshape(RL * CL, C)
    unit = x * inverse_rms(x)
    normed = (unit * gains).astype(BF16)
    u_ext[3 : RL + 3, 4 : CL + 4, :] = unit.reshape(RL, CL, C)
    projected = dot(normed, wqkv[...])
    q_loc[...] = (projected[:, 0:C] * 0.125).reshape(RL, CL, C)
    k_ext[3 : RL + 3, 4 : CL + 4, :] = projected[:, C : 2 * C].reshape(RL, CL, C)
    v_ext[3 : RL + 3, 4 : CL + 4, :] = projected[:, 2 * C : 3 * C].reshape(RL, CL, C)
    da_loc[...] = dot(cot[...].reshape(RL * CL, C), wout[...], NT).reshape(RL, CL, C)

    head0 = lax.broadcasted_iota(jnp.int32, (1, C), 1) < 64

    def two_heads(v):
        v = v.astype(BF16)
        zero = jnp.zeros_like(v)
        return jnp.concatenate([jnp.where(head0, v, zero), jnp.where(head0, zero, v)], axis=0)

    def block(row0, nr, col0, nc):
        kr, kc, nq = nr + 6, nc + 8, nr * nc
        lanes = 2 * nq
        keys = (slice(row0, row0 + kr), pl.ds(col0, kc))
        own = (slice(row0, row0 + nr), pl.ds(col0, nc))
        at = lax.broadcasted_iota(jnp.int32, (1, 1, lanes), 2) % nq
        q_row, q_col = at // nc, at % nc
        key_row = lax.broadcasted_iota(jnp.int32, (kr, 1, lanes), 0)
        key_col = lax.broadcasted_iota(jnp.int32, (1, kc, lanes), 1)
        image_row = gx * RL + row0 - 3 + key_row
        image_col = gy * CL + col0 - 4 + key_col
        row_bias = jnp.where(
            (key_row >= q_row) & (key_row <= q_row + 6) & (image_row >= 0) & (image_row < gxn * RL), 0.0, NEG
        )
        col_bias = jnp.where(
            (key_col >= q_col + 1) & (key_col <= q_col + 7) & (image_col >= 0) & (image_col < gyn * CL), 0.0, NEG
        )
        kw = k_ext[keys[0], keys[1], :].reshape(kr * kc, C).astype(BF16)
        vw = v_ext[keys[0], keys[1], :].reshape(kr * kc, C).astype(BF16)
        qb = two_heads(q_loc[own[0], own[1], :].reshape(nq, C))
        db = two_heads(da_loc[own[0], own[1], :].reshape(nq, C))
        scores = dot(kw, qb, NT).reshape(kr, kc, lanes)
        weights = jnp.exp(scores + row_bias + col_bias).reshape(kr * kc, lanes)
        totals = jnp.sum(weights, axis=0, keepdims=True)
        shares = weights * (1.0 / totals)
        shares_low = shares.astype(BF16)
        d_shares = dot(vw, db, NT)
        delta = jnp.sum(shares * d_shares, axis=0, keepdims=True)
        d_scores = (shares * (d_shares - delta)).astype(BF16)
        a2 = dot(shares_low, vw, TN)
        dq2 = dot(d_scores, kw, TN)
        att[own[0], own[1], :] = jnp.where(head0, a2[0:nq], a2[nq:]).reshape(nr, nc, C)
        dq[own[0], own[1], :] = jnp.where(head0, dq2[0:nq], dq2[nq:]).reshape(nr, nc, C)
        dk_ext[keys[0], keys[1], :] += dot(d_scores, qb).reshape(kr, kc, C)
        dv_ext[keys[0], keys[1], :] += dot(shares_low, db).reshape(kr, kc, C)

    def inner(j, carry):
        block(3, RL - 6, pl.multiple_of(j * 8, 8), 8)
        return carry

    lax.fori_loop(1, NB - 1, inner, 0, unroll=INNER_UNROLL)

    for copy, dst, _, come in halo:
        pl.when(come)(copy.wait_recv)

        @pl.when(jnp.logical_not(come))
        def _():
            dst[...] = jnp.zeros(dst.shape, BF16)

    rims = (
        (rx_rows[0].astype(F32), slice(0, 3), slice(4, CL + 4), slice(0, CL)),
        (rx_rows[1].astype(F32), slice(RL + 3, RE), slice(4, CL + 4), slice(0, CL)),
        (rx_cols[0].astype(F32)[:, 8:16], slice(3, RL + 3), slice(0, 4), slice(4, 8)),
        (rx_cols[1].astype(F32)[:, 0:8], slice(3, RL + 3), slice(CL + 4, CE), slice(0, 4)),
        (rx_corner[0].astype(F32)[:, 8:16], slice(0, 3), slice(0, 4), slice(4, 8)),
        (rx_corner[1].astype(F32)[:, 0:8], slice(0, 3), slice(CL + 4, CE), slice(0, 4)),
        (rx_corner[2].astype(F32)[:, 8:16], slice(RL + 3, RE), slice(0, 4), slice(4, 8)),
        (rx_corner[3].astype(F32)[:, 0:8], slice(RL + 3, RE), slice(CL + 4, CE), slice(0, 4)),
    )
    xh = jnp.concatenate([rim[0].reshape(-1, C) for rim in rims], axis=0)
    uh = xh * inverse_rms(xh)
    kvh = keyval(uh)
    start = 0
    for tokens, rsl, csl, used in rims:
        shape = tokens.shape
        n = shape[0] * shape[1]
        u_ext[rsl, csl, :] = uh[start : start + n].reshape(shape)[:, used]
        k_ext[rsl, csl, :] = kvh[start : start + n, 0:C].reshape(shape)[:, used]
        v_ext[rsl, csl, :] = kvh[start : start + n, C : 2 * C].reshape(shape)[:, used]
        start += n

    block(3, RL - 6, 0, 8)
    block(3, RL - 6, CL - 8, 8)

    def strips(j, carry):
        col0 = pl.multiple_of(j * STRIP, 8)
        block(0, 3, col0, STRIP)
        block(RL - 3, 3, col0, STRIP)
        return carry

    lax.fori_loop(0, CL // STRIP, strips, 0, unroll=STRIP_UNROLL)

    attended = att[...].reshape(RL * CL, C).astype(BF16)
    d_query = (dq[...] * 0.125).reshape(RL * CL, C).astype(BF16)
    cot_rows = cot[...].reshape(RL * CL, C)
    u = u_ext[...].reshape(RE * CE, C).astype(BF16)
    d_kv = jnp.concatenate(
        [dk_ext[...].reshape(RE * CE, C).astype(BF16), dv_ext[...].reshape(RE * CE, C).astype(BF16)], axis=-1
    )
    g_kv = dot(u, d_kv, TN)
    gsum[0:C, :] = dot(unit.astype(BF16), d_query, TN)
    gsum[C : 2 * C, :] = g_kv[:, 0:C]
    gsum[2 * C : 3 * C, :] = g_kv[:, C : 2 * C]
    gsum[3 * C : 4 * C, :] = dot(attended, cot_rows, TN)
    g16[...] = gsum[...].astype(BF16)
    for d in range(1, na):
        m, device = plane(d)
        pltpu.make_async_remote_copy(
            g16.at[pl.ds(pl.multiple_of(m * rows, rows), rows)],
            rs_rx.at[pl.ds((d - 1) * rows, rows)],
            a_send.at[0], a_recv.at[0], device_id=device, device_id_type=MESH,
        ).start()

    dn_ext[...] = dot(d_kv, wqkv[:, C : 3 * C], NT).reshape(RE, CE, C)
    pad_rows = jnp.zeros((8, C), F32)
    for i, lo in enumerate((0, RL + 3)):
        flat = dn_ext[lo : lo + 3].reshape(3 * CE, C)
        tx2_rows[i] = jnp.concatenate([flat, pad_rows], axis=0).astype(BF16)
        for k, left in enumerate((0, CL)):
            corner = dn_ext[lo : lo + 3, left : left + 8].reshape(24, C)
            tx2_corner[2 * i + k] = jnp.concatenate([corner, pad_rows], axis=0).astype(BF16)
    for k, left in enumerate((0, CL)):
        tx2_cols[k] = dn_ext[3 : RL + 3, left : left + 8].reshape(RL * 8, C).astype(BF16)
    back = []
    for i, (dr, dc) in enumerate(around):
        if dc == 0:
            n = 0 if dr < 0 else 1
            src, dst = tx2_rows.at[n], rx2_rows.at[n]
        elif dr == 0:
            n = 0 if dc < 0 else 1
            src, dst = tx2_cols.at[n], rx2_cols.at[n]
        else:
            n = (0 if dr < 0 else 2) + (0 if dc < 0 else 1)
            src, dst = tx2_corner.at[n], rx2_corner.at[n]
        copy = pltpu.make_async_remote_copy(
            src, dst, d_send.at[i], d_recv.at[i], device_id=beside(dr, dc), device_id_type=MESH
        )
        copy.start()
        back.append(copy)

    x = tok[...].astype(F32).reshape(RL * CL, C)
    out[...] = (x + dot(attended, wout[...])).astype(BF16).reshape(RL, CL, C)
    writes = [
        pltpu.make_async_copy(src, dst, out_sem.at[i])
        for i, (src, dst) in enumerate(
            ((out, out_hbm), (tgrad, tgrad_hbm), (qkvg, qkvg_hbm), (outg, outg_hbm), (gaing, gaing_hbm))
        )
    ]
    writes[0].start()
    for copy, _, to, _ in halo:
        pl.when(to)(copy.wait_send)

    wait_bytes(rs_rx, a_recv.at[0])
    mine = gsum[pl.ds(pl.multiple_of(me * rows, rows), rows), :]
    parts = rs_rx[...].astype(F32).reshape(na - 1, rows, C)
    z_rx[pl.ds(z, 1)] = (mine + jnp.sum(parts, axis=0)).astype(BF16)[None]
    for d in range(1, zn):
        pltpu.make_async_remote_copy(
            z_rx.at[z], z_rx.at[z],
            a_send.at[1], a_recv.at[1], device_id=column(d), device_id_type=MESH,
        ).start()

    for copy in back:
        copy.wait()
    sub = lax.broadcasted_iota(jnp.int32, (1, 8, 1), 1)
    tile = lax.broadcasted_iota(jnp.int32, (1, CE, 1), 1)
    middle = (tile >= 4) & (tile < CL + 4)

    def add(rsl, csl, rx, n, mask):
        shape = (rsl.stop - rsl.start, csl.stop - csl.start, C)
        more = rx[n].astype(F32)[0 : shape[0] * shape[1]].reshape(shape)
        dn_ext[rsl, csl, :] += jnp.where(mask, more, 0.0)

    first, last = slice(3, 6), slice(RL, RL + 3)
    left, right = slice(0, 8), slice(CL, CE)
    add(last, slice(0, CE), rx2_rows, 0, middle)
    add(first, slice(0, CE), rx2_rows, 1, middle)
    add(slice(3, RL + 3), right, rx2_cols, 0, sub < 4)
    add(slice(3, RL + 3), left, rx2_cols, 1, sub >= 4)
    add(last, right, rx2_corner, 0, sub < 4)
    add(last, left, rx2_corner, 1, sub >= 4)
    add(first, right, rx2_corner, 2, sub < 4)
    add(first, left, rx2_corner, 3, sub >= 4)
    d_normed = dot(d_query, wqkv[:, 0:C], NT) + dn_ext[3 : RL + 3, 4 : CL + 4, :].reshape(RL * CL, C)
    x = tok[...].astype(F32).reshape(RL * CL, C)
    r = inverse_rms(x)
    unit = x * r
    g = d_normed * gains
    mean = jnp.sum(g * unit, axis=-1, keepdims=True) * (1.0 / C)
    grads = cot_rows.astype(F32) + r * (g - unit * mean)
    tgrad[...] = grads.astype(BF16).reshape(RL, CL, C)
    writes[1].start()

    wait_bytes(z_rx.at[pl.ds(0, zn - 1)], a_recv.at[1])
    here = pl.ds(pl.multiple_of(me * rows, rows), rows)
    ag[here, :] = jnp.sum(z_rx[...].astype(F32), axis=0).astype(BF16)
    for d in range(1, na):
        m, device = plane(d)
        pltpu.make_async_remote_copy(
            ag.at[here], ag.at[here],
            a_send.at[2], a_recv.at[2], device_id=device, device_id_type=MESH,
        ).start()
    eye = lax.broadcasted_iota(jnp.int32, (C, C), 0) == lax.broadcasted_iota(jnp.int32, (C, C), 1)
    gain_col = jnp.sum(jnp.where(eye, gains, 0.0), axis=1, keepdims=True)
    wait_bytes(z_rx.at[pl.ds(0, zn - 1)], a_send.at[1])
    wait_bytes(rs_rx, a_send.at[0])
    wait_bytes(rs_rx, a_recv.at[2])
    factor = (gxn * RL * gyn * CL) ** (-0.5)
    total = jnp.zeros((C, C), F32)
    for i in range(3):
        piece = ag[i * C : (i + 1) * C, :].astype(F32) * factor
        qkvg[:, i * C : (i + 1) * C] = piece * gain_col
        total += piece * wqkv[:, i * C : (i + 1) * C].astype(F32)
    writes[2].start()
    outg[...] = ag[3 * C : 4 * C, :].astype(F32) * factor
    writes[3].start()
    gain_sum = jnp.sum(total, axis=1, keepdims=True)
    gaing[...] = jnp.sum(jnp.where(eye, gain_sum, 0.0), axis=0, keepdims=True)
    writes[4].start()
    wait_bytes(rs_rx, a_send.at[2])
    for write in writes:
        write.wait()


def finish(*refs):
    held, sem = refs[10:15], refs[15]
    reads = [pltpu.make_async_copy(refs[i], held[i], sem.at[0, i]) for i in range(5)]
    writes = [pltpu.make_async_copy(held[i], refs[5 + i], sem.at[1, i]) for i in range(5)]
    for read in reads:
        read.start()
    for read, write in zip(reads, writes):
        read.wait()
        write.start()
    for write in writes:
        write.wait()


def per_device(gxn, gyn, zn, tokens, norm_gain, qkv_weight, output_weight, cotangent):
    na = (gxn // zn) * gyn
    rows = 512 // na
    hbm = pl.BlockSpec(memory_space=pl.ANY)
    results = (
        jax.ShapeDtypeStruct((RL, CL, C), BF16),
        jax.ShapeDtypeStruct((RL, CL, C), BF16),
        jax.ShapeDtypeStruct((C, 3 * C), F32),
        jax.ShapeDtypeStruct((C, C), F32),
        jax.ShapeDtypeStruct((1, C), F32),
    )
    image = pltpu.VMEM((RL, CL, C), BF16)
    image32 = pltpu.VMEM((RL, CL, C), F32)
    ext32 = pltpu.VMEM((RE, CE, C), F32)
    dma = pltpu.SemaphoreType.DMA
    raw = pl.pallas_call(
        functools.partial(kernel, gxn, gyn, zn),
        out_shape=results,
        in_specs=[hbm] * 5,
        out_specs=(hbm,) * 5,
        scratch_shapes=[
            image,
            pltpu.VMEM((1, C), F32),
            pltpu.VMEM((C, 3 * C), BF16),
            pltpu.VMEM((C, C), BF16),
            image,
            image,
            image,
            pltpu.VMEM((C, 3 * C), F32),
            pltpu.VMEM((C, C), F32),
            pltpu.VMEM((1, C), F32),
            pltpu.VMEM((2, 3, CL, C), BF16),
            pltpu.VMEM((2, RL, 16, C), BF16),
            pltpu.VMEM((4, 3, 16, C), BF16),
            ext32, ext32, ext32, ext32, ext32, ext32,
            image32, image32, image32, image32,
            pltpu.VMEM((2, 224, C), BF16),
            pltpu.VMEM((2, RL * 8, C), BF16),
            pltpu.VMEM((4, 32, C), BF16),
            pltpu.VMEM((2, 224, C), BF16),
            pltpu.VMEM((2, RL * 8, C), BF16),
            pltpu.VMEM((4, 32, C), BF16),
            pltpu.VMEM((4 * C, C), F32),
            pltpu.VMEM((4 * C, C), BF16),
            pltpu.VMEM(((na - 1) * rows, C), BF16),
            pltpu.VMEM((zn, rows, C), BF16),
            pltpu.VMEM((4 * C, C), BF16),
            dma((5,)), dma((5,)), dma((8,)), dma((8,)), dma((8,)), dma((8,)), dma((3,)), dma((3,)),
        ],
        compiler_params=pltpu.CompilerParams(
            collective_id=0, has_side_effects=True, vmem_limit_bytes=60 << 20
        ),
    )(
        tokens.reshape(RL, CL, C),
        norm_gain.reshape(1, C),
        qkv_weight,
        output_weight,
        cotangent.reshape(RL, CL, C),
    )
    out, tgrad, qkvg, outg, gaing = pl.pallas_call(
        finish,
        out_shape=results,
        in_specs=[hbm] * 5,
        out_specs=(hbm,) * 5,
        scratch_shapes=[pltpu.VMEM(r.shape, r.dtype) for r in results] + [dma((2, 5))],
        compiler_params=pltpu.CompilerParams(vmem_limit_bytes=60 << 20),
    )(*raw)
    return (
        out.reshape(tokens.shape),
        tgrad.reshape(tokens.shape),
        qkvg,
        outg,
        gaing.reshape(C),
    )


def solution(mesh):
    gxn, gyn = mesh.shape["gx"], mesh.shape["gy"]
    image = P(None, "gx", "gy", None)
    return jax.shard_map(
        functools.partial(per_device, gxn, gyn, min(ZN, max(gxn // 4, 2))),
        mesh=mesh,
        in_specs=(image, P(), P(), P(), image),
        out_specs=(image, image, P(), P(), P()),
        check_vma=False,
    )
```

time: 46.8 us -> 37.4 us (0.80)
  local copies, waits for them, and re-layouts: 7.42 us -> 0 us
  Pallas kernels: 38.5 us -> 36.7 us
    unnamed x15 -> x0, local copies, waits for them, and re-layouts: 7.42 us -> none
    pallas_call x1 -> x2, Pallas kernels: 38.5 us -> 36.7 us  [the longest x1 34.8 us: per_device(): pl.pallas_call(functools.partial(kernel, gxn, gyn, zn), out_shape=results...]
where the time goes in v2:
time: 37.4 us; the launch traced here: 37.3 us
  Pallas kernels  36.7 us (98%)
  between operations  0.64 us (2%)
    pallas_call x1, Pallas kernels, per_device(): pl.pallas_call(functools.partial(kernel, gxn, gyn, zn), out_shape=results...  34.8 us
    pallas_call x1, Pallas kernels, per_device(): pl.pallas_call(finish, out_shape=results, in_specs=[hbm] * 5, out_specs=(...  1.91 us

profile of v2, /device:TPU:1, one launch (start us, length us, event | category | flops | bytes accessed | tf_op | source)
XLA Modules:
  0.0 37.3 jit_solution(651634527644780267)
XLA Ops:
  0.6 34.8 %shard_map.92 = (bf16[16,64,128]{2,1,0:T(8,128)(2,1)}, bf16[16,64,128]{2,1,0:T(8,128)(2,1)}, f32[128,384]{1,0:T(8,128)}, f32[128,128]{1,0:T(8,128)}, f32[1,128]{1,0:T(1,128)}) custom-call(bf16[16,64,128]{2,1,0:T(8,128)(2,1)} %bitcast.6, f32[1,128]{1,0:T(1,128)} %bitcast.8, bf16[128,384]{1,0:T(8,128)(2,1)} %wqkv_hbm.1, bf16[128,128]{1,0:T(8,128)(2,1)} %wout_hbm.1, ...), custom_call_target="tpu_custom_call" | custom-call | tf_op jit(solution)/shard_map/pallas_call | solution.py:386
  35.4 1.9 %shard_map.93 = (bf16[16,64,128]{2,1,0:T(8,128)(2,1)}, bf16[16,64,128]{2,1,0:T(8,128)(2,1)}, f32[128,384]{1,0:T(8,128)}, f32[128,128]{1,0:T(8,128)}, f32[1,128]{1,0:T(1,128)}) custom-call(bf16[16,64,128]{2,1,0:T(8,128)(2,1)} %get-tuple-element.15.refs_0_, bf16[16,64,128]{2,1,0:T(8,128)(2,1)} %get-tuple-element.16.refs_1_, ...), custom_call_target="tpu_custom_call" | custom-call | tf_op jit(solution)/shard_map/pallas_call | solution.py:430

commit v3 on v2

--- a/solution.py
+++ b/solution.py
@@ -16,8 +16,6 @@
 RE, CE = RL + 6, CL + 8
 NB = CL // 8
 STRIP = 32
-INNER_UNROLL = 6
-STRIP_UNROLL = 2
 NEG = -1e30
 ZN = 8
 
@@ -36,14 +34,14 @@
 def kernel(
     gxn, gyn, zn,
     tok_hbm, gain_hbm, wqkv_hbm, wout_hbm, cot_hbm,
-    out_hbm, tgrad_hbm, qkvg_hbm, outg_hbm, gaing_hbm,
+    out_hbm, tgrad_hbm, summed_hbm,
     tok, gain, wqkv, wout, cot,
-    out, tgrad, qkvg, outg, gaing,
+    out, tgrad,
     rx_rows, rx_cols, rx_corner,
     u_ext, k_ext, v_ext, dk_ext, dv_ext, dn_ext,
     q_loc, da_loc, att, dq,
     tx2_rows, tx2_cols, tx2_corner, rx2_rows, rx2_cols, rx2_corner,
-    gsum, g16, rs_rx, z_rx, ag,
+    gsum, g16, rs_rx, z_rx, own,
     in_sem, out_sem, h_send, h_recv, d_send, d_recv, a_send, a_recv,
 ):
     yn = gxn // zn
@@ -51,39 +49,30 @@
     rows = 512 // na
     gx = lax.axis_index("gx")
     gy = lax.axis_index("gy")
-    y, z = gx // zn, gx % zn
+    y, z = lax.div(gx, zn), lax.rem(gx, zn)
     me = y * gyn + gy
+    ys = [lax.rem(y + d, yn) * zn + z for d in range(yn)]
+    cs = [lax.rem(gy + d, gyn) for d in range(gyn)]
+    zs = [y * zn + lax.rem(z + d, zn) for d in range(zn)]
+
+    def far(d, n):
+        return min(d, n - d)
+
+    plane = sorted(
+        ((dy, dc) for dy in range(yn) for dc in range(gyn) if dy or dc),
+        key=lambda o: (-far(o[0], yn) - far(o[1], gyn) / 2, o),
+    )
+    column = sorted(range(1, zn), key=lambda d: (-far(d, zn), d))
 
     def beside(dr, dc):
-        return ((gx + dr + gxn) % gxn, (gy + dc + gyn) % gyn)
+        return (lax.rem(gx + (dr + gxn), gxn) if dr else gx, cs[dc % gyn])
 
     def exists(dr, dc):
         r, c = gx + dr, gy + dc
         return (r >= 0) & (r < gxn) & (c >= 0) & (c < gyn)
 
-    def plane(d):
-        m = (me + d) % na
-        return m, ((m // gyn) * zn + z, m % gyn)
-
-    def column(d):
-        return (y * zn + (z + d) % zn, gy)
-
     def wait_bytes(ref, sem):
         pltpu.make_async_copy(ref, ref, sem).wait()
-
-    around = [(dr, dc) for dr in (-1, 0, 1) for dc in (-1, 0, 1) if dr or dc]
-    barrier = pltpu.get_barrier_semaphore()
-
-    def greet(device):
-        pl.semaphore_signal(barrier, inc=1, device_id=device, device_id_type=MESH)
-
-    for dr, dc in around:
-        if dr:
-            greet(beside(dr, dc))
-    for d in range(1, zn):
-        greet(column(d))
-    for d in range(1, na):
-        greet(plane(d)[1])
 
     fetches = [
         pltpu.make_async_copy(src, dst, in_sem.at[i])
@@ -91,16 +80,29 @@
             ((tok_hbm, tok), (gain_hbm, gain), (wqkv_hbm, wqkv), (cot_hbm, cot), (wout_hbm, wout))
         )
     ]
+    around = [(dr, dc) for dr in (-1, 0, 1) for dc in (-1, 0, 1) if dr or dc]
+    barrier = pltpu.get_barrier_semaphore()
+
+    def greet(device):
+        pl.semaphore_signal(barrier, inc=1, device_id=device, device_id_type=MESH)
+
     for fetch in fetches:
         fetch.start()
-
+    for dr, dc in around:
+        if dr:
+            greet(beside(dr, dc))
+    for dy, dc in reversed(plane):
+        greet((ys[dy], cs[dc]))
+    for d in reversed(column):
+        greet((zs[d], gy))
+    fetches[0].wait()
     pl.semaphore_wait(barrier, 6 + (zn - 1) + (na - 1))
 
     halo = []
     for i, (dr, dc) in enumerate(around):
         rsl = slice(0, RL) if dr == 0 else (slice(0, 3) if dr < 0 else slice(RL - 3, RL))
         csl = slice(0, CL) if dc == 0 else (slice(0, 16) if dc < 0 else slice(CL - 16, CL))
-        src = tok_hbm.at[rsl, csl]
+        src = tok.at[rsl, csl]
         if dc == 0:
             dst = rx_rows.at[0 if dr > 0 else 1]
         elif dr == 0:
@@ -114,7 +116,7 @@
     for copy, dst, to, _ in halo:
         pl.when(to)(copy.start)
 
-    for fetch in fetches:
+    for fetch in fetches[1:]:
         fetch.wait()
     dk_ext[...] = jnp.zeros_like(dk_ext)
     dv_ext[...] = jnp.zeros_like(dv_ext)
@@ -177,11 +179,8 @@
         dk_ext[keys[0], keys[1], :] += dot(d_scores, qb).reshape(kr, kc, C)
         dv_ext[keys[0], keys[1], :] += dot(shares_low, db).reshape(kr, kc, C)
 
-    def inner(j, carry):
-        block(3, RL - 6, pl.multiple_of(j * 8, 8), 8)
-        return carry
-
-    lax.fori_loop(1, NB - 1, inner, 0, unroll=INNER_UNROLL)
+    for j in range(1, NB - 1):
+        block(3, RL - 6, j * 8, 8)
 
     for copy, dst, _, come in halo:
         pl.when(come)(copy.wait_recv)
@@ -215,13 +214,9 @@
     block(3, RL - 6, 0, 8)
     block(3, RL - 6, CL - 8, 8)
 
-    def strips(j, carry):
-        col0 = pl.multiple_of(j * STRIP, 8)
+    for col0 in range(0, CL, STRIP):
         block(0, 3, col0, STRIP)
         block(RL - 3, 3, col0, STRIP)
-        return carry
-
-    lax.fori_loop(0, CL // STRIP, strips, 0, unroll=STRIP_UNROLL)
 
     attended = att[...].reshape(RL * CL, C).astype(BF16)
     d_query = (dq[...] * 0.125).reshape(RL * CL, C).astype(BF16)
@@ -236,12 +231,13 @@
     gsum[2 * C : 3 * C, :] = g_kv[:, C : 2 * C]
     gsum[3 * C : 4 * C, :] = dot(attended, cot_rows, TN)
     g16[...] = gsum[...].astype(BF16)
-    for d in range(1, na):
-        m, device = plane(d)
+    bases = [lax.rem(y + d, yn) * gyn for d in range(yn)]
+    for i, (dy, dc) in enumerate(plane):
+        m = bases[dy] + cs[dc]
         pltpu.make_async_remote_copy(
             g16.at[pl.ds(pl.multiple_of(m * rows, rows), rows)],
-            rs_rx.at[pl.ds((d - 1) * rows, rows)],
-            a_send.at[0], a_recv.at[0], device_id=device, device_id_type=MESH,
+            rs_rx.at[pl.ds(i * rows, rows)],
+            a_send.at[0], a_recv.at[0], device_id=(ys[dy], cs[dc]), device_id_type=MESH,
         ).start()
 
     dn_ext[...] = dot(d_kv, wqkv[:, C : 3 * C], NT).reshape(RE, CE, C)
@@ -273,10 +269,11 @@
 
     x = tok[...].astype(F32).reshape(RL * CL, C)
     out[...] = (x + dot(attended, wout[...])).astype(BF16).reshape(RL, CL, C)
+    here = pl.ds(pl.multiple_of(me * rows, rows), rows)
     writes = [
         pltpu.make_async_copy(src, dst, out_sem.at[i])
         for i, (src, dst) in enumerate(
-            ((out, out_hbm), (tgrad, tgrad_hbm), (qkvg, qkvg_hbm), (outg, outg_hbm), (gaing, gaing_hbm))
+            ((out, out_hbm), (tgrad, tgrad_hbm), (own, summed_hbm.at[here]))
         )
     ]
     writes[0].start()
@@ -287,10 +284,10 @@
     mine = gsum[pl.ds(pl.multiple_of(me * rows, rows), rows), :]
     parts = rs_rx[...].astype(F32).reshape(na - 1, rows, C)
     z_rx[pl.ds(z, 1)] = (mine + jnp.sum(parts, axis=0)).astype(BF16)[None]
-    for d in range(1, zn):
+    for d in column:
         pltpu.make_async_remote_copy(
             z_rx.at[z], z_rx.at[z],
-            a_send.at[1], a_recv.at[1], device_id=column(d), device_id_type=MESH,
+            a_send.at[1], a_recv.at[1], device_id=(zs[d], gy), device_id_type=MESH,
         ).start()
 
     for copy in back:
@@ -325,45 +322,48 @@
     writes[1].start()
 
     wait_bytes(z_rx.at[pl.ds(0, zn - 1)], a_recv.at[1])
-    here = pl.ds(pl.multiple_of(me * rows, rows), rows)
-    ag[here, :] = jnp.sum(z_rx[...].astype(F32), axis=0).astype(BF16)
-    for d in range(1, na):
-        m, device = plane(d)
+    own[...] = jnp.sum(z_rx[...].astype(F32), axis=0).astype(BF16)
+    for dy, dc in plane:
         pltpu.make_async_remote_copy(
-            ag.at[here], ag.at[here],
-            a_send.at[2], a_recv.at[2], device_id=device, device_id_type=MESH,
+            own, summed_hbm.at[here],
+            a_send.at[2], a_recv.at[2], device_id=(ys[dy], cs[dc]), device_id_type=MESH,
         ).start()
-    eye = lax.broadcasted_iota(jnp.int32, (C, C), 0) == lax.broadcasted_iota(jnp.int32, (C, C), 1)
-    gain_col = jnp.sum(jnp.where(eye, gains, 0.0), axis=1, keepdims=True)
+    writes[2].start()
     wait_bytes(z_rx.at[pl.ds(0, zn - 1)], a_send.at[1])
     wait_bytes(rs_rx, a_send.at[0])
+    for write in writes:
+        write.wait()
     wait_bytes(rs_rx, a_recv.at[2])
-    factor = (gxn * RL * gyn * CL) ** (-0.5)
+    wait_bytes(rs_rx, a_send.at[2])
+
+
+def finish(
+    factor, out, tgrad, summed, gain, wqkv, out_hbm, tgrad_hbm, qkvg_hbm, outg_hbm, gaing_hbm,
+    out_v, tgrad_v, summed_v, gain_v, wqkv_v, qkvg, outg, gaing, r_sem, w_sem,
+):
+    held = ((summed, summed_v), (gain, gain_v), (wqkv, wqkv_v), (out, out_v), (tgrad, tgrad_v))
+    reads = [pltpu.make_async_copy(src, dst, r_sem.at[i]) for i, (src, dst) in enumerate(held)]
+    made = ((qkvg, qkvg_hbm), (outg, outg_hbm), (gaing, gaing_hbm), (out_v, out_hbm), (tgrad_v, tgrad_hbm))
+    writes = [pltpu.make_async_copy(src, dst, w_sem.at[i]) for i, (src, dst) in enumerate(made)]
+    for read in reads:
+        read.start()
+    eye = lax.broadcasted_iota(jnp.int32, (C, C), 0) == lax.broadcasted_iota(jnp.int32, (C, C), 1)
+    for read in reads:
+        read.wait()
+    writes[3].start()
+    writes[4].start()
+    gain_col = jnp.sum(jnp.where(eye, gain_v[...], 0.0), axis=1, keepdims=True)
     total = jnp.zeros((C, C), F32)
     for i in range(3):
-        piece = ag[i * C : (i + 1) * C, :].astype(F32) * factor
+        piece = summed_v[i * C : (i + 1) * C, :].astype(F32) * factor
         qkvg[:, i * C : (i + 1) * C] = piece * gain_col
-        total += piece * wqkv[:, i * C : (i + 1) * C].astype(F32)
-    writes[2].start()
-    outg[...] = ag[3 * C : 4 * C, :].astype(F32) * factor
-    writes[3].start()
+        total += piece * wqkv_v[:, i * C : (i + 1) * C].astype(F32)
+    writes[0].start()
+    outg[...] = summed_v[3 * C : 4 * C, :].astype(F32) * factor
+    writes[1].start()
     gain_sum = jnp.sum(total, axis=1, keepdims=True)
     gaing[...] = jnp.sum(jnp.where(eye, gain_sum, 0.0), axis=0, keepdims=True)
-    writes[4].start()
-    wait_bytes(rs_rx, a_send.at[2])
-    for write in writes:
-        write.wait()
-
-
-def finish(*refs):
-    held, sem = refs[10:15], refs[15]
-    reads = [pltpu.make_async_copy(refs[i], held[i], sem.at[0, i]) for i in range(5)]
-    writes = [pltpu.make_async_copy(held[i], refs[5 + i], sem.at[1, i]) for i in range(5)]
-    for read in reads:
-        read.start()
-    for read, write in zip(reads, writes):
-        read.wait()
-        write.start()
+    writes[2].start()
     for write in writes:
         write.wait()
 
@@ -371,10 +371,10 @@
 def per_device(gxn, gyn, zn, tokens, norm_gain, qkv_weight, output_weight, cotangent):
     na = (gxn // zn) * gyn
     rows = 512 // na
+    gain_row = norm_gain.reshape(1, C)
     hbm = pl.BlockSpec(memory_space=pl.ANY)
-    results = (
-        jax.ShapeDtypeStruct((RL, CL, C), BF16),
-        jax.ShapeDtypeStruct((RL, CL, C), BF16),
+    images = (jax.ShapeDtypeStruct((RL, CL, C), BF16),) * 2
+    results = images + (
         jax.ShapeDtypeStruct((C, 3 * C), F32),
         jax.ShapeDtypeStruct((C, C), F32),
         jax.ShapeDtypeStruct((1, C), F32),
@@ -385,9 +385,9 @@
     dma = pltpu.SemaphoreType.DMA
     raw = pl.pallas_call(
         functools.partial(kernel, gxn, gyn, zn),
-        out_shape=results,
+        out_shape=images + (jax.ShapeDtypeStruct((4 * C, C), BF16),),
         in_specs=[hbm] * 5,
-        out_specs=(hbm,) * 5,
+        out_specs=(hbm,) * 3,
         scratch_shapes=[
             image,
             pltpu.VMEM((1, C), F32),
@@ -396,9 +396,6 @@
             image,
             image,
             image,
-            pltpu.VMEM((C, 3 * C), F32),
-            pltpu.VMEM((C, C), F32),
-            pltpu.VMEM((1, C), F32),
             pltpu.VMEM((2, 3, CL, C), BF16),
             pltpu.VMEM((2, RL, 16, C), BF16),
             pltpu.VMEM((4, 3, 16, C), BF16),
@@ -414,27 +411,38 @@
             pltpu.VMEM((4 * C, C), BF16),
             pltpu.VMEM(((na - 1) * rows, C), BF16),
             pltpu.VMEM((zn, rows, C), BF16),
-            pltpu.VMEM((4 * C, C), BF16),
-            dma((5,)), dma((5,)), dma((8,)), dma((8,)), dma((8,)), dma((8,)), dma((3,)), dma((3,)),
+            pltpu.VMEM((rows, C), BF16),
+            dma((5,)), dma((3,)), dma((8,)), dma((8,)), dma((8,)), dma((8,)), dma((3,)), dma((3,)),
         ],
         compiler_params=pltpu.CompilerParams(
             collective_id=0, has_side_effects=True, vmem_limit_bytes=60 << 20
         ),
     )(
         tokens.reshape(RL, CL, C),
-        norm_gain.reshape(1, C),
+        gain_row,
         qkv_weight,
         output_weight,
         cotangent.reshape(RL, CL, C),
     )
     out, tgrad, qkvg, outg, gaing = pl.pallas_call(
-        finish,
+        functools.partial(finish, (gxn * RL * gyn * CL) ** (-0.5)),
         out_shape=results,
         in_specs=[hbm] * 5,
         out_specs=(hbm,) * 5,
-        scratch_shapes=[pltpu.VMEM(r.shape, r.dtype) for r in results] + [dma((2, 5))],
+        scratch_shapes=[
+            image,
+            image,
+            pltpu.VMEM((4 * C, C), BF16),
+            pltpu.VMEM((1, C), F32),
+            pltpu.VMEM((C, 3 * C), BF16),
+            pltpu.VMEM((C, 3 * C), F32),
+            pltpu.VMEM((C, C), F32),
+            pltpu.VMEM((1, C), F32),
+            dma((5,)),
+            dma((5,)),
+        ],
         compiler_params=pltpu.CompilerParams(vmem_limit_bytes=60 << 20),
-    )(*raw)
+    )(*raw, gain_row, qkv_weight)
     return (
         out.reshape(tokens.shape),
         tgrad.reshape(tokens.shape),

time: 37.4 us -> 35.8 us (0.957)
  Pallas kernels: 36.7 us -> 35.1 us
    pallas_call x2, Pallas kernels: 36.7 us -> 35.1 us  [the longest x1 33 us: per_device(): pl.pallas_call(functools.partial(kernel, gxn, gyn, zn), out_shape=images...]
where the time goes in v3:
time: 35.8 us; the launch traced here: 35.7 us
  Pallas kernels  35.1 us (98%)
  between operations  0.64 us (2%)
    pallas_call x1, Pallas kernels, per_device(): pl.pallas_call(functools.partial(kernel, gxn, gyn, zn), out_shape=images...  33 us
    pallas_call x1, Pallas kernels, per_device(): pl.pallas_call(functools.partial(finish, (gxn * RL * gyn * CL) ** (-0.5))...  2.12 us

profile of v3, /device:TPU:1, one launch (start us, length us, event | category | flops | bytes accessed | tf_op | source)
XLA Modules:
  0.0 35.7 jit_solution(14095581046933851984)
XLA Ops:
  0.6 33.0 %shard_map.92 = (bf16[16,64,128]{2,1,0:T(8,128)(2,1)}, bf16[16,64,128]{2,1,0:T(8,128)(2,1)}, bf16[512,128]{1,0:T(8,128)(2,1)}) custom-call(bf16[16,64,128]{2,1,0:T(8,128)(2,1)} %bitcast.6, f32[1,128]{1,0:T(1,128)} %bitcast.8, bf16[128,384]{1,0:T(8,128)(2,1)} %wqkv.1, bf16[128,128]{1,0:T(8,128)(2,1)} %wout_hbm.1, bf16[16,64,128]{2,1,0:T(8,128)(2,1)} %bitcast.7), custom_call_target="tpu_custom_call" | custom-call | tf_op jit(solution)/shard_map/pallas_call | solution.py:386
  33.6 2.1 %shard_map.93 = (bf16[16,64,128]{2,1,0:T(8,128)(2,1)}, bf16[16,64,128]{2,1,0:T(8,128)(2,1)}, f32[128,384]{1,0:T(8,128)}, f32[128,128]{1,0:T(8,128)}, f32[1,128]{1,0:T(1,128)}) custom-call(bf16[16,64,128]{2,1,0:T(8,128)(2,1)} %get-tuple-element.13.out, bf16[16,64,128]{2,1,0:T(8,128)(2,1)} %get-tuple-element.14.tgrad, ...), custom_call_target="tpu_custom_call" | custom-call | tf_op jit(solution)/shard_map/pallas_call | solution.py:427

commit v4 on v3

--- a/solution.py
+++ b/solution.py
@@ -15,7 +15,7 @@
 RL, CL = 16, 64
 RE, CE = RL + 6, CL + 8
 NB = CL // 8
-STRIP = 32
+STRIP = 16
 NEG = -1e30
 ZN = 8
 
@@ -37,7 +37,7 @@
     out_hbm, tgrad_hbm, summed_hbm,
     tok, gain, wqkv, wout, cot,
     out, tgrad,
-    rx_rows, rx_cols, rx_corner,
+    tx_cols, tx_corner, rx_rows, rx_cols, rx_corner,
     u_ext, k_ext, v_ext, dk_ext, dv_ext, dn_ext,
     q_loc, da_loc, att, dq,
     tx2_rows, tx2_cols, tx2_corner, rx2_rows, rx2_cols, rx2_corner,
@@ -80,7 +80,7 @@
             ((tok_hbm, tok), (gain_hbm, gain), (wqkv_hbm, wqkv), (cot_hbm, cot), (wout_hbm, wout))
         )
     ]
-    around = [(dr, dc) for dr in (-1, 0, 1) for dc in (-1, 0, 1) if dr or dc]
+    around = [(-1, 0), (1, 0), (-1, -1), (-1, 1), (1, -1), (1, 1), (0, -1), (0, 1)]
     barrier = pltpu.get_barrier_semaphore()
 
     def greet(device):
@@ -98,22 +98,38 @@
     fetches[0].wait()
     pl.semaphore_wait(barrier, 6 + (zn - 1) + (na - 1))
 
+    def packed(v):
+        if v.shape[0] == 3:
+            v = jnp.concatenate([v, v[0:1]], axis=0)
+        half = v.shape[0] // 2
+        return jnp.concatenate([v[0:half], v[half:]], axis=1).reshape(half * 8, C).astype(BF16)
+
+    def unpacked(v):
+        v = v.reshape(-1, 8, C)
+        return jnp.concatenate([v[:, 0:4], v[:, 4:8]], axis=0)
+
+    def place(dr, dc):
+        return 2 * (dr > 0) + (dc > 0)
+
     halo = []
     for i, (dr, dc) in enumerate(around):
-        rsl = slice(0, RL) if dr == 0 else (slice(0, 3) if dr < 0 else slice(RL - 3, RL))
-        csl = slice(0, CL) if dc == 0 else (slice(0, 16) if dc < 0 else slice(CL - 16, CL))
-        src = tok.at[rsl, csl]
         if dc == 0:
-            dst = rx_rows.at[0 if dr > 0 else 1]
+            src, dst = tok.at[slice(0, 3) if dr < 0 else slice(RL - 3, RL)], rx_rows.at[place(dr, 0) // 2]
         elif dr == 0:
-            dst = rx_cols.at[0 if dc > 0 else 1]
+            src, dst = tx_cols.at[place(0, dc)], rx_cols.at[place(0, dc)]
         else:
-            dst = rx_corner.at[(0 if dr > 0 else 2) + (0 if dc > 0 else 1)]
+            src, dst = tx_corner.at[place(dr, dc)], rx_corner.at[place(dr, dc)]
         copy = pltpu.make_async_remote_copy(
             src, dst, h_send.at[i], h_recv.at[i], device_id=beside(dr, dc), device_id_type=MESH
         )
         halo.append((copy, dst, exists(dr, dc), exists(-dr, -dc)))
-    for copy, dst, to, _ in halo:
+    for copy, _, to, _ in halo[0:2]:
+        pl.when(to)(copy.start)
+    for k, csl in enumerate((slice(0, 4), slice(CL - 4, CL))):
+        for n, rsl in enumerate((slice(0, 3), slice(RL - 3, RL))):
+            tx_corner[2 * n + k] = packed(tok[rsl].astype(F32)[:, csl])
+        tx_cols[k] = packed(tok[...].astype(F32)[:, csl])
+    for copy, _, to, _ in halo[2:]:
         pl.when(to)(copy.start)
 
     for fetch in fetches[1:]:
@@ -143,44 +159,55 @@
         zero = jnp.zeros_like(v)
         return jnp.concatenate([jnp.where(head0, v, zero), jnp.where(head0, zero, v)], axis=0)
 
-    def block(row0, nr, col0, nc):
-        kr, kc, nq = nr + 6, nc + 8, nr * nc
-        lanes = 2 * nq
-        keys = (slice(row0, row0 + kr), pl.ds(col0, kc))
-        own = (slice(row0, row0 + nr), pl.ds(col0, nc))
-        at = lax.broadcasted_iota(jnp.int32, (1, 1, lanes), 2) % nq
-        q_row, q_col = at // nc, at % nc
-        key_row = lax.broadcasted_iota(jnp.int32, (kr, 1, lanes), 0)
-        key_col = lax.broadcasted_iota(jnp.int32, (1, kc, lanes), 1)
-        image_row = gx * RL + row0 - 3 + key_row
-        image_col = gy * CL + col0 - 4 + key_col
-        row_bias = jnp.where(
-            (key_row >= q_row) & (key_row <= q_row + 6) & (image_row >= 0) & (image_row < gxn * RL), 0.0, NEG
-        )
-        col_bias = jnp.where(
-            (key_col >= q_col + 1) & (key_col <= q_col + 7) & (image_col >= 0) & (image_col < gyn * CL), 0.0, NEG
-        )
-        kw = k_ext[keys[0], keys[1], :].reshape(kr * kc, C).astype(BF16)
-        vw = v_ext[keys[0], keys[1], :].reshape(kr * kc, C).astype(BF16)
-        qb = two_heads(q_loc[own[0], own[1], :].reshape(nq, C))
-        db = two_heads(da_loc[own[0], own[1], :].reshape(nq, C))
-        scores = dot(kw, qb, NT).reshape(kr, kc, lanes)
-        weights = jnp.exp(scores + row_bias + col_bias).reshape(kr * kc, lanes)
-        totals = jnp.sum(weights, axis=0, keepdims=True)
-        shares = weights * (1.0 / totals)
-        shares_low = shares.astype(BF16)
-        d_shares = dot(vw, db, NT)
-        delta = jnp.sum(shares * d_shares, axis=0, keepdims=True)
-        d_scores = (shares * (d_shares - delta)).astype(BF16)
-        a2 = dot(shares_low, vw, TN)
-        dq2 = dot(d_scores, kw, TN)
-        att[own[0], own[1], :] = jnp.where(head0, a2[0:nq], a2[nq:]).reshape(nr, nc, C)
-        dq[own[0], own[1], :] = jnp.where(head0, dq2[0:nq], dq2[nq:]).reshape(nr, nc, C)
-        dk_ext[keys[0], keys[1], :] += dot(d_scores, qb).reshape(kr, kc, C)
-        dv_ext[keys[0], keys[1], :] += dot(shares_low, db).reshape(kr, kc, C)
-
-    for j in range(1, NB - 1):
-        block(3, RL - 6, j * 8, 8)
+    def blocks(places):
+        each = []
+        for row0, nr, col0, nc in places:
+            kr, kc, nq = nr + 6, nc + 8, nr * nc
+            keys = (slice(row0, row0 + kr), slice(col0, col0 + kc))
+            own_at = (slice(row0, row0 + nr), slice(col0, col0 + nc))
+            each.append((row0, nr, col0, nc, kr, kc, nq, keys, own_at))
+        kws = [k_ext[b[7][0], b[7][1], :].reshape(b[4] * b[5], C).astype(BF16) for b in each]
+        vws = [v_ext[b[7][0], b[7][1], :].reshape(b[4] * b[5], C).astype(BF16) for b in each]
+        qbs = [two_heads(q_loc[b[8][0], b[8][1], :].reshape(b[6], C)) for b in each]
+        dbs = [two_heads(da_loc[b[8][0], b[8][1], :].reshape(b[6], C)) for b in each]
+        scores = [dot(kw, qb, NT) for kw, qb in zip(kws, qbs)]
+        d_shares = [dot(vw, db, NT) for vw, db in zip(vws, dbs)]
+        shares, lows = [], []
+        for (row0, nr, col0, nc, kr, kc, nq, _, _), score in zip(each, scores):
+            lanes = 2 * nq
+            at = lax.broadcasted_iota(jnp.int32, (1, 1, lanes), 2) % nq
+            q_row, q_col = at // nc, at % nc
+            key_row = lax.broadcasted_iota(jnp.int32, (kr, 1, lanes), 0)
+            key_col = lax.broadcasted_iota(jnp.int32, (1, kc, lanes), 1)
+            image_row = gx * RL + row0 - 3 + key_row
+            image_col = gy * CL + col0 - 4 + key_col
+            row_bias = jnp.where(
+                (key_row >= q_row) & (key_row <= q_row + 6) & (image_row >= 0) & (image_row < gxn * RL), 0.0, NEG
+            )
+            col_bias = jnp.where(
+                (key_col >= q_col + 1) & (key_col <= q_col + 7) & (image_col >= 0) & (image_col < gyn * CL), 0.0, NEG
+            )
+            weights = jnp.exp(score.reshape(kr, kc, lanes) + row_bias + col_bias).reshape(kr * kc, lanes)
+            totals = jnp.sum(weights, axis=0, keepdims=True)
+            shares.append(weights * (1.0 / totals))
+            lows.append(shares[-1].astype(BF16))
+        a2s = [dot(low, vw, TN) for low, vw in zip(lows, vws)]
+        dvs = [dot(low, db) for low, db in zip(lows, dbs)]
+        d_scores = []
+        for share, d_share in zip(shares, d_shares):
+            delta = jnp.sum(share * d_share, axis=0, keepdims=True)
+            d_scores.append((share * (d_share - delta)).astype(BF16))
+        dq2s = [dot(ds, kw, TN) for ds, kw in zip(d_scores, kws)]
+        dks = [dot(ds, qb) for ds, qb in zip(d_scores, qbs)]
+        for b, a2, dq2, dk, dv in zip(each, a2s, dq2s, dks, dvs):
+            _, nr, _, nc, kr, kc, nq, keys, own_at = b
+            att[own_at[0], own_at[1], :] = jnp.where(head0, a2[0:nq], a2[nq:]).reshape(nr, nc, C)
+            dq[own_at[0], own_at[1], :] = jnp.where(head0, dq2[0:nq], dq2[nq:]).reshape(nr, nc, C)
+            dk_ext[keys[0], keys[1], :] += dk.reshape(kr, kc, C)
+            dv_ext[keys[0], keys[1], :] += dv.reshape(kr, kc, C)
+
+    for j in range(1, NB - 1, 2):
+        blocks([(3, RL - 6, j * 8, 8), (3, RL - 6, j * 8 + 8, 8)])
 
     for copy, dst, _, come in halo:
         pl.when(come)(copy.wait_recv)
@@ -189,34 +216,36 @@
         def _():
             dst[...] = jnp.zeros(dst.shape, BF16)
 
+    above, below = slice(0, 3), slice(RL + 3, RE)
+    level, far_left, far_right = slice(3, RL + 3), slice(0, 4), slice(CL + 4, CE)
+    inside = slice(4, CL + 4)
     rims = (
-        (rx_rows[0].astype(F32), slice(0, 3), slice(4, CL + 4), slice(0, CL)),
-        (rx_rows[1].astype(F32), slice(RL + 3, RE), slice(4, CL + 4), slice(0, CL)),
-        (rx_cols[0].astype(F32)[:, 8:16], slice(3, RL + 3), slice(0, 4), slice(4, 8)),
-        (rx_cols[1].astype(F32)[:, 0:8], slice(3, RL + 3), slice(CL + 4, CE), slice(0, 4)),
-        (rx_corner[0].astype(F32)[:, 8:16], slice(0, 3), slice(0, 4), slice(4, 8)),
-        (rx_corner[1].astype(F32)[:, 0:8], slice(0, 3), slice(CL + 4, CE), slice(0, 4)),
-        (rx_corner[2].astype(F32)[:, 8:16], slice(RL + 3, RE), slice(0, 4), slice(4, 8)),
-        (rx_corner[3].astype(F32)[:, 0:8], slice(RL + 3, RE), slice(CL + 4, CE), slice(0, 4)),
-    )
-    xh = jnp.concatenate([rim[0].reshape(-1, C) for rim in rims], axis=0)
+        (rx_rows[1].reshape(-1, C), above, inside),
+        (rx_rows[0].reshape(-1, C), below, inside),
+        (rx_cols[1], level, far_left),
+        (rx_cols[0], level, far_right),
+        (rx_corner[3], above, far_left),
+        (rx_corner[2], above, far_right),
+        (rx_corner[1], below, far_left),
+        (rx_corner[0], below, far_right),
+    )
+    xh = jnp.concatenate([rim[0].astype(F32) for rim in rims], axis=0)
     uh = xh * inverse_rms(xh)
     kvh = keyval(uh)
     start = 0
-    for tokens, rsl, csl, used in rims:
-        shape = tokens.shape
-        n = shape[0] * shape[1]
-        u_ext[rsl, csl, :] = uh[start : start + n].reshape(shape)[:, used]
-        k_ext[rsl, csl, :] = kvh[start : start + n, 0:C].reshape(shape)[:, used]
-        v_ext[rsl, csl, :] = kvh[start : start + n, C : 2 * C].reshape(shape)[:, used]
+    for tokens, rsl, csl in rims:
+        n = tokens.shape[0]
+        for ref, v in ((u_ext, uh), (k_ext, kvh[:, 0:C]), (v_ext, kvh[:, C:])):
+            piece = v[start : start + n]
+            piece = piece.reshape(3, CL, C) if csl is inside else unpacked(piece)
+            ref[rsl, csl, :] = piece[0 : rsl.stop - rsl.start]
         start += n
 
-    block(3, RL - 6, 0, 8)
-    block(3, RL - 6, CL - 8, 8)
-
+    edge = [(3, RL - 6, 0, 8), (3, RL - 6, CL - 8, 8)]
     for col0 in range(0, CL, STRIP):
-        block(0, 3, col0, STRIP)
-        block(RL - 3, 3, col0, STRIP)
+        edge += [(0, 3, col0, STRIP), (RL - 3, 3, col0, STRIP)]
+    blocks(edge[0:5])
+    blocks(edge[5:10])
 
     attended = att[...].reshape(RL * CL, C).astype(BF16)
     d_query = (dq[...] * 0.125).reshape(RL * CL, C).astype(BF16)
@@ -241,26 +270,20 @@
         ).start()
 
     dn_ext[...] = dot(d_kv, wqkv[:, C : 3 * C], NT).reshape(RE, CE, C)
-    pad_rows = jnp.zeros((8, C), F32)
-    for i, lo in enumerate((0, RL + 3)):
-        flat = dn_ext[lo : lo + 3].reshape(3 * CE, C)
-        tx2_rows[i] = jnp.concatenate([flat, pad_rows], axis=0).astype(BF16)
-        for k, left in enumerate((0, CL)):
-            corner = dn_ext[lo : lo + 3, left : left + 8].reshape(24, C)
-            tx2_corner[2 * i + k] = jnp.concatenate([corner, pad_rows], axis=0).astype(BF16)
-    for k, left in enumerate((0, CL)):
-        tx2_cols[k] = dn_ext[3 : RL + 3, left : left + 8].reshape(RL * 8, C).astype(BF16)
+    for i, rsl in enumerate((above, below)):
+        tx2_rows[i] = dn_ext[rsl, 4 : CL + 4, :].astype(BF16)
+        for k, csl in enumerate((far_left, far_right)):
+            tx2_corner[2 * i + k] = packed(dn_ext[rsl, csl, :])
+    for k, csl in enumerate((far_left, far_right)):
+        tx2_cols[k] = packed(dn_ext[level, csl, :])
     back = []
     for i, (dr, dc) in enumerate(around):
         if dc == 0:
-            n = 0 if dr < 0 else 1
-            src, dst = tx2_rows.at[n], rx2_rows.at[n]
+            src, dst = tx2_rows.at[place(dr, 0) // 2], rx2_rows.at[place(dr, 0) // 2]
         elif dr == 0:
-            n = 0 if dc < 0 else 1
-            src, dst = tx2_cols.at[n], rx2_cols.at[n]
+            src, dst = tx2_cols.at[place(0, dc)], rx2_cols.at[place(0, dc)]
         else:
-            n = (0 if dr < 0 else 2) + (0 if dc < 0 else 1)
-            src, dst = tx2_corner.at[n], rx2_corner.at[n]
+            src, dst = tx2_corner.at[place(dr, dc)], rx2_corner.at[place(dr, dc)]
         copy = pltpu.make_async_remote_copy(
             src, dst, d_send.at[i], d_recv.at[i], device_id=beside(dr, dc), device_id_type=MESH
         )
@@ -292,25 +315,14 @@
 
     for copy in back:
         copy.wait()
-    sub = lax.broadcasted_iota(jnp.int32, (1, 8, 1), 1)
-    tile = lax.broadcasted_iota(jnp.int32, (1, CE, 1), 1)
-    middle = (tile >= 4) & (tile < CL + 4)
-
-    def add(rsl, csl, rx, n, mask):
-        shape = (rsl.stop - rsl.start, csl.stop - csl.start, C)
-        more = rx[n].astype(F32)[0 : shape[0] * shape[1]].reshape(shape)
-        dn_ext[rsl, csl, :] += jnp.where(mask, more, 0.0)
-
     first, last = slice(3, 6), slice(RL, RL + 3)
-    left, right = slice(0, 8), slice(CL, CE)
-    add(last, slice(0, CE), rx2_rows, 0, middle)
-    add(first, slice(0, CE), rx2_rows, 1, middle)
-    add(slice(3, RL + 3), right, rx2_cols, 0, sub < 4)
-    add(slice(3, RL + 3), left, rx2_cols, 1, sub >= 4)
-    add(last, right, rx2_corner, 0, sub < 4)
-    add(last, left, rx2_corner, 1, sub >= 4)
-    add(first, right, rx2_corner, 2, sub < 4)
-    add(first, left, rx2_corner, 3, sub >= 4)
+    left, right = slice(4, 8), slice(CL, CL + 4)
+    dn_ext[last, inside, :] += rx2_rows[0].astype(F32)
+    dn_ext[first, inside, :] += rx2_rows[1].astype(F32)
+    dn_ext[level, right, :] += unpacked(rx2_cols[0].astype(F32))
+    dn_ext[level, left, :] += unpacked(rx2_cols[1].astype(F32))
+    for n, (rsl, csl) in enumerate(((last, right), (last, left), (first, right), (first, left))):
+        dn_ext[rsl, csl, :] += unpacked(rx2_corner[n].astype(F32))[0:3]
     d_normed = dot(d_query, wqkv[:, 0:C], NT) + dn_ext[3 : RL + 3, 4 : CL + 4, :].reshape(RL * CL, C)
     x = tok[...].astype(F32).reshape(RL * CL, C)
     r = inverse_rms(x)
@@ -383,6 +395,8 @@
     image32 = pltpu.VMEM((RL, CL, C), F32)
     ext32 = pltpu.VMEM((RE, CE, C), F32)
     dma = pltpu.SemaphoreType.DMA
+    cols = pltpu.VMEM((2, RL * 4, C), BF16)
+    corners = pltpu.VMEM((4, 16, C), BF16)
     raw = pl.pallas_call(
         functools.partial(kernel, gxn, gyn, zn),
         out_shape=images + (jax.ShapeDtypeStruct((4 * C, C), BF16),),
@@ -396,17 +410,19 @@
             image,
             image,
             image,
+            cols,
+            corners,
             pltpu.VMEM((2, 3, CL, C), BF16),
-            pltpu.VMEM((2, RL, 16, C), BF16),
-            pltpu.VMEM((4, 3, 16, C), BF16),
+            cols,
+            corners,
             ext32, ext32, ext32, ext32, ext32, ext32,
             image32, image32, image32, image32,
-            pltpu.VMEM((2, 224, C), BF16),
-            pltpu.VMEM((2, RL * 8, C), BF16),
-            pltpu.VMEM((4, 32, C), BF16),
-            pltpu.VMEM((2, 224, C), BF16),
-            pltpu.VMEM((2, RL * 8, C), BF16),
-            pltpu.VMEM((4, 32, C), BF16),
+            pltpu.VMEM((2, 3, CL, C), BF16),
+            cols,
+            corners,
+            pltpu.VMEM((2, 3, CL, C), BF16),
+            cols,
+            corners,
             pltpu.VMEM((4 * C, C), F32),
             pltpu.VMEM((4 * C, C), BF16),
             pltpu.VMEM(((na - 1) * rows, C), BF16),

time: 35.8 us -> 34.5 us (0.964)
  Pallas kernels: 35.1 us -> 33.7 us
    pallas_call x1, Pallas kernels: 33 us -> 31.6 us  [per_device(): pl.pallas_call(functools.partial(kernel, gxn, gyn, zn), out_shape=images...]
where the time goes in v4:
time: 34.5 us; the launch traced here: 34.3 us
  Pallas kernels  33.7 us (98%)
  between operations  0.64 us (2%)
    pallas_call x1, Pallas kernels, per_device(): pl.pallas_call(functools.partial(kernel, gxn, gyn, zn), out_shape=images...  31.6 us
    pallas_call x1, Pallas kernels, per_device(): pl.pallas_call(functools.partial(finish, (gxn * RL * gyn * CL) ** (-0.5))...  2.12 us

profile of v4, /device:TPU:1, one launch (start us, length us, event | category | flops | bytes accessed | tf_op | source)
XLA Modules:
  0.0 34.3 jit_solution(9706874532325006568)
XLA Ops:
  0.6 31.6 %shard_map.92 = (bf16[16,64,128]{2,1,0:T(8,128)(2,1)}, bf16[16,64,128]{2,1,0:T(8,128)(2,1)}, bf16[512,128]{1,0:T(8,128)(2,1)}) custom-call(bf16[16,64,128]{2,1,0:T(8,128)(2,1)} %bitcast.6, f32[1,128]{1,0:T(1,128)} %bitcast.8, bf16[128,384]{1,0:T(8,128)(2,1)} %wqkv.1, bf16[128,128]{1,0:T(8,128)(2,1)} %wout_hbm.1, bf16[16,64,128]{2,1,0:T(8,128)(2,1)} %bitcast.7), custom_call_target="tpu_custom_call" | custom-call | tf_op jit(solution)/shard_map/pallas_call | solution.py:400
  32.2 2.1 %shard_map.93 = (bf16[16,64,128]{2,1,0:T(8,128)(2,1)}, bf16[16,64,128]{2,1,0:T(8,128)(2,1)}, f32[128,384]{1,0:T(8,128)}, f32[128,128]{1,0:T(8,128)}, f32[1,128]{1,0:T(1,128)}) custom-call(bf16[16,64,128]{2,1,0:T(8,128)(2,1)} %get-tuple-element.13.out, bf16[16,64,128]{2,1,0:T(8,128)(2,1)} %get-tuple-element.14.tgrad, ...), custom_call_target="tpu_custom_call" | custom-call | tf_op jit(solution)/shard_map/pallas_call | solution.py:443

commit v5 on v4

--- a/solution.py
+++ b/solution.py
@@ -88,13 +88,13 @@
 
     for fetch in fetches:
         fetch.start()
+    for d in column:
+        greet((zs[d], gy))
+    for dy, dc in plane:
+        greet((ys[dy], cs[dc]))
     for dr, dc in around:
         if dr:
             greet(beside(dr, dc))
-    for dy, dc in reversed(plane):
-        greet((ys[dy], cs[dc]))
-    for d in reversed(column):
-        greet((zs[d], gy))
     fetches[0].wait()
     pl.semaphore_wait(barrier, 6 + (zn - 1) + (na - 1))
 
@@ -212,10 +212,6 @@
     for copy, dst, _, come in halo:
         pl.when(come)(copy.wait_recv)
 
-        @pl.when(jnp.logical_not(come))
-        def _():
-            dst[...] = jnp.zeros(dst.shape, BF16)
-
     above, below = slice(0, 3), slice(RL + 3, RE)
     level, far_left, far_right = slice(3, RL + 3), slice(0, 4), slice(CL + 4, CE)
     inside = slice(4, CL + 4)
@@ -229,7 +225,10 @@
         (rx_corner[1], below, far_left),
         (rx_corner[0], below, far_right),
     )
-    xh = jnp.concatenate([rim[0].astype(F32) for rim in rims], axis=0)
+    has = ((-1, 0), (1, 0), (0, -1), (0, 1), (-1, -1), (-1, 1), (1, -1), (1, 1))
+    xh = jnp.concatenate(
+        [jnp.where(exists(dr, dc), rim[0].astype(F32), 0.0) for rim, (dr, dc) in zip(rims, has)], axis=0
+    )
     uh = xh * inverse_rms(xh)
     kvh = keyval(uh)
     start = 0
@@ -360,20 +359,22 @@
     for read in reads:
         read.start()
     eye = lax.broadcasted_iota(jnp.int32, (C, C), 0) == lax.broadcasted_iota(jnp.int32, (C, C), 1)
-    for read in reads:
-        read.wait()
-    writes[3].start()
-    writes[4].start()
-    gain_col = jnp.sum(jnp.where(eye, gain_v[...], 0.0), axis=1, keepdims=True)
+    reads[1].wait()
+    gain_col = jnp.sum(jnp.where(eye, gain_v[...], 0.0), axis=1, keepdims=True) * factor
+    reads[0].wait()
+    reads[2].wait()
+    outg[...] = summed_v[3 * C : 4 * C, :].astype(F32) * factor
+    writes[1].start()
     total = jnp.zeros((C, C), F32)
     for i in range(3):
-        piece = summed_v[i * C : (i + 1) * C, :].astype(F32) * factor
+        piece = summed_v[i * C : (i + 1) * C, :].astype(F32)
         qkvg[:, i * C : (i + 1) * C] = piece * gain_col
         total += piece * wqkv_v[:, i * C : (i + 1) * C].astype(F32)
     writes[0].start()
-    outg[...] = summed_v[3 * C : 4 * C, :].astype(F32) * factor
-    writes[1].start()
-    gain_sum = jnp.sum(total, axis=1, keepdims=True)
+    for i in (3, 4):
+        reads[i].wait()
+        writes[i].start()
+    gain_sum = jnp.sum(total, axis=1, keepdims=True) * factor
     gaing[...] = jnp.sum(jnp.where(eye, gain_sum, 0.0), axis=0, keepdims=True)
     writes[2].start()
     for write in writes:

time: 34.5 us -> 33.9 us (0.983)
  Pallas kernels: 33.7 us -> 33.1 us
    pallas_call x1, Pallas kernels: 31.6 us -> 31.1 us  [per_device(): pl.pallas_call(functools.partial(kernel, gxn, gyn, zn), out_shape=images...]
where the time goes in v5:
time: 33.9 us; the launch traced here: 33.7 us
  Pallas kernels  33.1 us (98%)
  between operations  0.64 us (2%)
    pallas_call x1, Pallas kernels, per_device(): pl.pallas_call(functools.partial(kernel, gxn, gyn, zn), out_shape=images...  31.1 us
    pallas_call x1, Pallas kernels, per_device(): pl.pallas_call(functools.partial(finish, (gxn * RL * gyn * CL) ** (-0.5))...  1.96 us

profile of v5, /device:TPU:1, one launch (start us, length us, event | category | flops | bytes accessed | tf_op | source)
XLA Modules:
  0.0 33.7 jit_solution(8208107916906844305)
XLA Ops:
  0.6 31.1 %shard_map.92 = (bf16[16,64,128]{2,1,0:T(8,128)(2,1)}, bf16[16,64,128]{2,1,0:T(8,128)(2,1)}, bf16[512,128]{1,0:T(8,128)(2,1)}) custom-call(bf16[16,64,128]{2,1,0:T(8,128)(2,1)} %bitcast.6, f32[1,128]{1,0:T(1,128)} %bitcast.8, bf16[128,384]{1,0:T(8,128)(2,1)} %wqkv.1, bf16[128,128]{1,0:T(8,128)(2,1)} %wout_hbm.1, bf16[16,64,128]{2,1,0:T(8,128)(2,1)} %bitcast.7), custom_call_target="tpu_custom_call" | custom-call | tf_op jit(solution)/shard_map/pallas_call | solution.py:401
  31.8 2.0 %shard_map.93 = (bf16[16,64,128]{2,1,0:T(8,128)(2,1)}, bf16[16,64,128]{2,1,0:T(8,128)(2,1)}, f32[128,384]{1,0:T(8,128)}, f32[128,128]{1,0:T(8,128)}, f32[1,128]{1,0:T(1,128)}) custom-call(bf16[16,64,128]{2,1,0:T(8,128)(2,1)} %get-tuple-element.13.out, bf16[16,64,128]{2,1,0:T(8,128)(2,1)} %get-tuple-element.14.tgrad, ...), custom_call_target="tpu_custom_call" | custom-call | tf_op jit(solution)/shard_map/pallas_call | solution.py:444

commit v6 on v5

--- a/solution.py
+++ b/solution.py
@@ -189,7 +189,8 @@
             )
             weights = jnp.exp(score.reshape(kr, kc, lanes) + row_bias + col_bias).reshape(kr * kc, lanes)
             totals = jnp.sum(weights, axis=0, keepdims=True)
-            shares.append(weights * (1.0 / totals))
+            scale = jnp.where(totals > 1.0, 2.0**-64, 1.0)
+            shares.append(weights * (1.0 / (totals * scale)) * scale)
             lows.append(shares[-1].astype(BF16))
         a2s = [dot(low, vw, TN) for low, vw in zip(lows, vws)]
         dvs = [dot(low, db) for low, db in zip(lows, dbs)]

time: 33.9 us -> 34 us (level)
  no operation moved by 1% of the time
where the time goes in v6:
time: 34 us; the launch traced here: 33.9 us
  Pallas kernels  33.2 us (98%)
  between operations  0.64 us (2%)
    pallas_call x1, Pallas kernels, per_device(): pl.pallas_call(functools.partial(kernel, gxn, gyn, zn), out_shape=images...  31.3 us
    pallas_call x1, Pallas kernels, per_device(): pl.pallas_call(functools.partial(finish, (gxn * RL * gyn * CL) ** (-0.5))...  1.96 us

profile of v6, /device:TPU:1, one launch (start us, length us, event | category | flops | bytes accessed | tf_op | source)
XLA Modules:
  0.0 33.9 jit_solution(2877968648443607753)
XLA Ops:
  0.6 31.3 %shard_map.92 = (bf16[16,64,128]{2,1,0:T(8,128)(2,1)}, bf16[16,64,128]{2,1,0:T(8,128)(2,1)}, bf16[512,128]{1,0:T(8,128)(2,1)}) custom-call(bf16[16,64,128]{2,1,0:T(8,128)(2,1)} %bitcast.6, f32[1,128]{1,0:T(1,128)} %bitcast.8, bf16[128,384]{1,0:T(8,128)(2,1)} %wqkv.1, bf16[128,128]{1,0:T(8,128)(2,1)} %wout_hbm.1, bf16[16,64,128]{2,1,0:T(8,128)(2,1)} %bitcast.7), custom_call_target="tpu_custom_call" | custom-call | tf_op jit(solution)/shard_map/pallas_call | solution.py:402
  31.9 2.0 %shard_map.93 = (bf16[16,64,128]{2,1,0:T(8,128)(2,1)}, bf16[16,64,128]{2,1,0:T(8,128)(2,1)}, f32[128,384]{1,0:T(8,128)}, f32[128,128]{1,0:T(8,128)}, f32[1,128]{1,0:T(1,128)}) custom-call(bf16[16,64,128]{2,1,0:T(8,128)(2,1)} %get-tuple-element.13.out, bf16[16,64,128]{2,1,0:T(8,128)(2,1)} %get-tuple-element.14.tgrad, ...), custom_call_target="tpu_custom_call" | custom-call | tf_op jit(solution)/shard_map/pallas_call | solution.py:445

commit v7 on v6

--- a/solution.py
+++ b/solution.py
@@ -41,7 +41,7 @@
     u_ext, k_ext, v_ext, dk_ext, dv_ext, dn_ext,
     q_loc, da_loc, att, dq,
     tx2_rows, tx2_cols, tx2_corner, rx2_rows, rx2_cols, rx2_corner,
-    gsum, g16, rs_rx, z_rx, own,
+    unit_t, u_t, gsum, g16, rs_rx, z_rx, own,
     in_sem, out_sem, h_send, h_recv, d_send, d_recv, a_send, a_recv,
 ):
     yn = gxn // zn
@@ -96,8 +96,6 @@
         if dr:
             greet(beside(dr, dc))
     fetches[0].wait()
-    pl.semaphore_wait(barrier, 6 + (zn - 1) + (na - 1))
-
     def packed(v):
         if v.shape[0] == 3:
             v = jnp.concatenate([v, v[0:1]], axis=0)
@@ -107,6 +105,13 @@
     def unpacked(v):
         v = v.reshape(-1, 8, C)
         return jnp.concatenate([v[:, 0:4], v[:, 4:8]], axis=0)
+
+    for k, csl in enumerate((slice(0, 4), slice(CL - 4, CL))):
+        for n, rsl in enumerate((slice(0, 3), slice(RL - 3, RL))):
+            tx_corner[2 * n + k] = packed(tok[rsl].astype(F32)[:, csl])
+        tx_cols[k] = packed(tok[...].astype(F32)[:, csl])
+
+    pl.semaphore_wait(barrier, 6 + (zn - 1) + (na - 1))
 
     def place(dr, dc):
         return 2 * (dr > 0) + (dc > 0)
@@ -123,13 +128,7 @@
             src, dst, h_send.at[i], h_recv.at[i], device_id=beside(dr, dc), device_id_type=MESH
         )
         halo.append((copy, dst, exists(dr, dc), exists(-dr, -dc)))
-    for copy, _, to, _ in halo[0:2]:
-        pl.when(to)(copy.start)
-    for k, csl in enumerate((slice(0, 4), slice(CL - 4, CL))):
-        for n, rsl in enumerate((slice(0, 3), slice(RL - 3, RL))):
-            tx_corner[2 * n + k] = packed(tok[rsl].astype(F32)[:, csl])
-        tx_cols[k] = packed(tok[...].astype(F32)[:, csl])
-    for copy, _, to, _ in halo[2:]:
+    for copy, _, to, _ in halo:
         pl.when(to)(copy.start)
 
     for fetch in fetches[1:]:
@@ -146,6 +145,7 @@
     unit = x * inverse_rms(x)
     normed = (unit * gains).astype(BF16)
     u_ext[3 : RL + 3, 4 : CL + 4, :] = unit.reshape(RL, CL, C)
+    unit_t[...] = unit.T.astype(BF16)
     projected = dot(normed, wqkv[...])
     q_loc[...] = (projected[:, 0:C] * 0.125).reshape(RL, CL, C)
     k_ext[3 : RL + 3, 4 : CL + 4, :] = projected[:, C : 2 * C].reshape(RL, CL, C)
@@ -210,52 +210,56 @@
     for j in range(1, NB - 1, 2):
         blocks([(3, RL - 6, j * 8, 8), (3, RL - 6, j * 8 + 8, 8)])
 
-    for copy, dst, _, come in halo:
-        pl.when(come)(copy.wait_recv)
 
     above, below = slice(0, 3), slice(RL + 3, RE)
     level, far_left, far_right = slice(3, RL + 3), slice(0, 4), slice(CL + 4, CE)
     inside = slice(4, CL + 4)
     rims = (
-        (rx_rows[1].reshape(-1, C), above, inside),
-        (rx_rows[0].reshape(-1, C), below, inside),
-        (rx_cols[1], level, far_left),
-        (rx_cols[0], level, far_right),
-        (rx_corner[3], above, far_left),
-        (rx_corner[2], above, far_right),
-        (rx_corner[1], below, far_left),
-        (rx_corner[0], below, far_right),
+        (rx_rows, 1, above, inside),
+        (rx_rows, 0, below, inside),
+        (rx_cols, 1, level, far_left),
+        (rx_cols, 0, level, far_right),
+        (rx_corner, 3, above, far_left),
+        (rx_corner, 2, above, far_right),
+        (rx_corner, 1, below, far_left),
+        (rx_corner, 0, below, far_right),
     )
     has = ((-1, 0), (1, 0), (0, -1), (0, 1), (-1, -1), (-1, 1), (1, -1), (1, 1))
-    xh = jnp.concatenate(
-        [jnp.where(exists(dr, dc), rim[0].astype(F32), 0.0) for rim, (dr, dc) in zip(rims, has)], axis=0
-    )
-    uh = xh * inverse_rms(xh)
-    kvh = keyval(uh)
-    start = 0
-    for tokens, rsl, csl in rims:
-        n = tokens.shape[0]
-        for ref, v in ((u_ext, uh), (k_ext, kvh[:, 0:C]), (v_ext, kvh[:, C:])):
-            piece = v[start : start + n]
-            piece = piece.reshape(3, CL, C) if csl is inside else unpacked(piece)
-            ref[rsl, csl, :] = piece[0 : rsl.stop - rsl.start]
-        start += n
-
-    edge = [(3, RL - 6, 0, 8), (3, RL - 6, CL - 8, 8)]
-    for col0 in range(0, CL, STRIP):
-        edge += [(0, 3, col0, STRIP), (RL - 3, 3, col0, STRIP)]
-    blocks(edge[0:5])
-    blocks(edge[5:10])
+
+    def fill(copies, wanted):
+        for copy, _, _, come in copies:
+            pl.when(come)(copy.wait_recv)
+        some = [(rims[n][0][rims[n][1]].reshape(-1, C), *rims[n][2:], has[n]) for n in wanted]
+        xh = jnp.concatenate(
+            [jnp.where(exists(*at), v.astype(F32), 0.0) for v, _, _, at in some], axis=0
+        )
+        uh = xh * inverse_rms(xh)
+        kvh = keyval(uh)
+        start = 0
+        for tokens, rsl, csl, _ in some:
+            n = tokens.shape[0]
+            for ref, v in ((u_ext, uh), (k_ext, kvh[:, 0:C]), (v_ext, kvh[:, C:])):
+                piece = v[start : start + n]
+                piece = piece.reshape(3, CL, C) if csl is inside else unpacked(piece)
+                ref[rsl, csl, :] = piece[0 : rsl.stop - rsl.start]
+            start += n
+
+    fill(halo[6:8], (2, 3))
+    blocks([(3, RL - 6, 0, 8), (3, RL - 6, CL - 8, 8)])
+    fill(halo[0:6], (0, 1, 4, 5, 6, 7))
+    strips = [(row0, 3, col0, STRIP) for col0 in range(0, CL, STRIP) for row0 in (0, RL - 3)]
+    u_t[...] = u_ext[...].reshape(RE * CE, C).T.astype(BF16)
+    blocks(strips[0:4])
+    blocks(strips[4:8])
 
     attended = att[...].reshape(RL * CL, C).astype(BF16)
     d_query = (dq[...] * 0.125).reshape(RL * CL, C).astype(BF16)
     cot_rows = cot[...].reshape(RL * CL, C)
-    u = u_ext[...].reshape(RE * CE, C).astype(BF16)
     d_kv = jnp.concatenate(
         [dk_ext[...].reshape(RE * CE, C).astype(BF16), dv_ext[...].reshape(RE * CE, C).astype(BF16)], axis=-1
     )
-    g_kv = dot(u, d_kv, TN)
-    gsum[0:C, :] = dot(unit.astype(BF16), d_query, TN)
+    g_kv = dot(u_t[...], d_kv)
+    gsum[0:C, :] = dot(unit_t[...], d_query)
     gsum[C : 2 * C, :] = g_kv[:, 0:C]
     gsum[2 * C : 3 * C, :] = g_kv[:, C : 2 * C]
     gsum[3 * C : 4 * C, :] = dot(attended, cot_rows, TN)
@@ -425,6 +429,8 @@
             pltpu.VMEM((2, 3, CL, C), BF16),
             cols,
             corners,
+            pltpu.VMEM((C, RL * CL), BF16),
+            pltpu.VMEM((C, RE * CE), BF16),
             pltpu.VMEM((4 * C, C), F32),
             pltpu.VMEM((4 * C, C), BF16),
             pltpu.VMEM(((na - 1) * rows, C), BF16),

time: 34 us -> 33.7 us (level)
  no operation moved by 1% of the time
where the time goes in v7:
time: 33.7 us; the launch traced here: 33.5 us
  Pallas kernels  32.9 us (98%)
  between operations  0.64 us (2%)
    pallas_call x1, Pallas kernels, per_device(): pl.pallas_call(functools.partial(kernel, gxn, gyn, zn), out_shape=images...  30.9 us
    pallas_call x1, Pallas kernels, per_device(): pl.pallas_call(functools.partial(finish, (gxn * RL * gyn * CL) ** (-0.5))...  1.96 us

profile of v7, /device:TPU:1, one launch (start us, length us, event | category | flops | bytes accessed | tf_op | source)
XLA Modules:
  0.0 33.5 jit_solution(17890841147686233291)
XLA Ops:
  0.6 30.9 %shard_map.92 = (bf16[16,64,128]{2,1,0:T(8,128)(2,1)}, bf16[16,64,128]{2,1,0:T(8,128)(2,1)}, bf16[512,128]{1,0:T(8,128)(2,1)}) custom-call(bf16[16,64,128]{2,1,0:T(8,128)(2,1)} %bitcast.6, f32[1,128]{1,0:T(1,128)} %bitcast.8, bf16[128,384]{1,0:T(8,128)(2,1)} %wqkv.1, bf16[128,128]{1,0:T(8,128)(2,1)} %wout_hbm.1, bf16[16,64,128]{2,1,0:T(8,128)(2,1)} %bitcast.7), custom_call_target="tpu_custom_call" | custom-call | tf_op jit(solution)/shard_map/pallas_call | solution.py:406
  31.6 2.0 %shard_map.93 = (bf16[16,64,128]{2,1,0:T(8,128)(2,1)}, bf16[16,64,128]{2,1,0:T(8,128)(2,1)}, f32[128,384]{1,0:T(8,128)}, f32[128,128]{1,0:T(8,128)}, f32[1,128]{1,0:T(1,128)}) custom-call(bf16[16,64,128]{2,1,0:T(8,128)(2,1)} %get-tuple-element.13.out, bf16[16,64,128]{2,1,0:T(8,128)(2,1)} %get-tuple-element.14.tgrad, ...), custom_call_target="tpu_custom_call" | custom-call | tf_op jit(solution)/shard_map/pallas_call | solution.py:451
